TPU v7x, 32 devices: a whole 2x2x4 slice. The times are simulated.
32 devices in a mesh: pole: 2 (over x), row: 16 (over z, y, core).
Axes of the slice: x: 2, y: 2, z: 4, core: 2. Of those that a mesh axis runs over, the one named last changes fastest.
Arguments:
- ainv_root: float32 [4, 512, 512], P('pole', 'row'), parts along dimension 0, as said below
- pattern: int32 [4, 4], replicated, may hold values 0 or 1
- panel_top: float32 [4, 2048, 128], P('pole', 'row'), parts along dimension 0, may hold values from -0.25 to 0.25
- inv_top: float32 [4, 512, 128], P('pole', 'row'), parts along dimension 0, may hold values from -6 to 6
- panel_mid: float32 [4, 4096, 128], P('pole', 'row'), parts along dimension 0, may hold values from -0.25 to 0.25
- link_mid: float32 [4, 1024, 128], P('pole', 'row'), parts along dimension 0, may hold values from -0.5 to 0.5
- inv_mid: float32 [4, 1024, 128], P('pole', 'row'), parts along dimension 0, may hold values from -6 to 6
- panel_leaf: float32 [4, 24576, 128], P('pole', 'row'), parts along dimension 0, may hold values from -0.25 to 0.25
- link_leaf_mid: float32 [4, 6144, 128], P('pole', 'row'), parts along dimension 0, may hold values from -0.5 to 0.5
- link_leaf_top: float32 [4, 6144, 128], P('pole', 'row'), parts along dimension 0, may hold values from -0.5 to 0.5
- inv_leaf: float32 [4, 6144, 128], P('pole', 'row'), parts along dimension 0, may hold values from -6 to 6
Outputs:
- col_top: float32 [4, 2048, 128], P('pole', 'row'), parts along dimension 0
- diag_top: float32 [4, 512, 128], P('pole', 'row'), parts along dimension 0
- col_mid: float32 [4, 4096, 128], P('pole', 'row'), parts along dimension 0
- cross_mid: float32 [4, 1024, 128], P('pole', 'row'), parts along dimension 0
- diag_mid: float32 [4, 1024, 128], P('pole', 'row'), parts along dimension 0
- col_leaf: float32 [4, 24576, 128], P('pole', 'row'), parts along dimension 0
- cross_leaf_mid: float32 [4, 6144, 128], P('pole', 'row'), parts along dimension 0
- cross_leaf_top: float32 [4, 6144, 128], P('pole', 'row'), parts along dimension 0
- diag_leaf: float32 [4, 6144, 128], P('pole', 'row'), parts along dimension 0
There are 2 independent parts, one for each index of `pole`. A program takes and returns all parts, laid end to end along the dimension named above; an argument that names none is the same for every part. Nothing has to cross between parts.
Inputs may be any that keep to these rules, and one draw needn't show every extreme that they name: ainv_root is complex symmetric: ainv_root[c, i, k] equals ainv_root[c, k, i].
All inputs are finite; a program needn't handle non-finite values.
Results may differ from a plain program's by a relative error of at most 0.00009.
Values sent between devices are 32-bit elements; how exact they have to be, the bound alone decides.
No kernel may reach another device: no remote copies, remote signals or barrier semaphores. Data moves between devices by JAX's collectives and lax.ppermute only.
A program may use at most 64 MiB of HBM per device.

v0:
```python
import jax
import jax.numpy as jnp
from jax import lax
from jax.experimental import pallas as pl
from jax.experimental.pallas import tpu as pltpu
from jax.sharding import PartitionSpec as P

F32 = jnp.float32
BF16 = jnp.bfloat16
ANY = pl.BlockSpec(memory_space=pl.ANY)
VMEM = pl.BlockSpec(memory_space=pltpu.VMEM)


def swap(x, apart):
    return lax.ppermute(x, "row", [(i, i ^ apart) for i in range(lax.axis_size("row"))])


def swap_by_core(x, apart_even, apart_odd):
    return lax.ppermute(
        x,
        "row",
        [(i, i ^ (apart_odd if i & 1 else apart_even)) for i in range(lax.axis_size("row"))],
    )


def halves(x):
    hi = x.astype(BF16)
    return hi, (x - hi.astype(F32)).astype(BF16)


def mm(a, b):
    return jnp.dot(a, b, preferred_element_type=F32)


def mm3(ah, al, bh, bl):
    return mm(ah, bh) + (mm(ah, bl) + mm(al, bh))


def at(start, size):
    return pl.ds(pl.multiple_of(start, size), size)


def in_hbm(x):
    return pltpu.with_memory_space_constraint(x, pltpu.HBM)


def own_plane(device, planes):
    return device // 4 if planes else device * 0


def pack_kernel(
    pat, a_hbm, a_other, t_hbm, i_hbm, pm_hbm, lm_hbm, im_hbm,
    z1, z2, z3, mine_top, mine_mid, masks, a, pat_s, sem,
):
    device = lax.axis_index("row")
    core = device % 2
    plane = device // 4
    pairs = (
        (a_hbm, a), (pat, pat_s),
        (t_hbm, mine_top.at[:, 0:128, :]), (i_hbm, mine_top.at[:, 128:160, :]),
        (pm_hbm, mine_mid.at[:, 0:256, :]), (lm_hbm, mine_mid.at[:, 256:320, :]),
        (im_hbm, mine_mid.at[:, 320:384, :]),
    )
    copies = [pltpu.make_async_copy(src, dst, sem.at[n]) for n, (src, dst) in enumerate(pairs)]
    for copy in copies:
        copy.start()
    for n, (ref, which) in enumerate(((a_other, 1 - core), (a, core))):
        if n == 1:
            copies[0].wait()
        rows = at(which * 32, 32)

        def block(apart):
            return ref[:, :, at((plane ^ apart) * 128, 128)]

        same = block(0)
        z1[:, rows, 0:128] = same
        z1[:, rows, 128:256] = block(3)
        z1[:, rows, 256:384] = block(2)
        z2[:, rows, 0:128] = same
        z2[:, rows, 128:256] = block(1)
        z3[:, rows, :] = same
    copies[1].wait()
    for r in range(4):
        masks[r : r + 1, :] = jnp.full((1, 128), pat_s[plane, plane ^ r], jnp.int32).astype(F32)
    masks[4:8, :] = jnp.zeros((4, 128), F32)
    for copy in copies[2:]:
        copy.wait()


def pack(pattern, a, a_other, *mine):
    shapes = [(2, 64, 384), (2, 64, 256), (2, 64, 128), (2, 160, 128), (2, 384, 128), (8, 128)]
    return pl.pallas_call(
        pack_kernel,
        out_shape=tuple(jax.ShapeDtypeStruct(s, F32) for s in shapes),
        in_specs=[ANY, ANY, VMEM] + [ANY] * 5,
        out_specs=(VMEM,) * len(shapes),
        scratch_shapes=[pltpu.VMEM(a.shape, F32), pltpu.SMEM(pattern.shape, jnp.int32), pltpu.SemaphoreType.DMA((7,))],
        compiler_params=pltpu.CompilerParams(vmem_limit_bytes=4 << 20),
        name="pack_sent",
    )(in_hbm(pattern), in_hbm(a), a_other, *(in_hbm(x) for x in mine))


def put_rhs(ref_h, ref_l, row, re, im):
    rh, rl = halves(re)
    ih, il = halves(im)
    for ref, r, i in ((ref_h, rh, ih), (ref_l, rl, il)):
        ref[row : row + 128, 0:128] = r
        ref[row : row + 128, 128:256] = i
        ref[row + 128 : row + 256, 0:128] = -i
        ref[row + 128 : row + 256, 128:256] = r


def put_pair(ref_h, ref_l, row, col, re, im):
    n = re.shape[0]
    rh, rl = halves(re)
    ih, il = halves(im)
    for ref, r, i in ((ref_h, rh, ih), (ref_l, rl, il)):
        ref[row : row + n, col : col + 128] = r
        ref[row : row + n, col + 128 : col + 256] = i


def put_transposed(ref_h, ref_l, row, r, re, im):
    for part, x in ((0, re), (128, im)):
        xh, xl = halves(x.T)
        ref_h[row + part : row + part + 128, r * 128 : r * 128 + 128] = xh
        ref_l[row + part : row + part + 128, r * 128 : r * 128 + 128] = xl


def make_front_kernel(planes, leaves):
    def kernel(
        mask_ref, top0, top1, top2, top3, mid0, mid1, panel, link_c, link_e, inv,
        x_h, x_l, tt_h, tt_l, tl_h, tl_l, base_top, base_leaf,
        l_s, b_s, t0_s, am_s, d_s, g_s, lc_s, le_s, li_s,
        lhs_h, lhs_l, ra_h, ra_l, rq_h, rq_l, aux_h, aux_l, rhs_h, rhs_l, rrs_h, rrs_l, auxl_h, auxl_l, sem,
    ):
        device = lax.axis_index("row")
        plane = own_plane(device, planes)
        quarter = device % 4
        half = device % 2
        copies = []

        def fetch(src, dst):
            copy = pltpu.make_async_copy(src, dst, sem.at[len(copies)])
            copy.start()
            copies.append(copy)
            return copy

        def rel(supernode):
            return at((supernode ^ plane) * 128, 128)

        links = [fetch(link_c, lc_s), fetch(link_e, le_s)]
        panels = [fetch(panel.at[:, j * 512 : j * 512 + 512, :], g_s.at[:, j * 512 : j * 512 + 512, :]) for j in range(leaves)]
        fetch(inv, li_s)
        for k, ref in enumerate((top0, top1, top2, top3)):
            l_s[:, rel(quarter ^ k), :] = ref[:, 0:128, :]
            t0_s[:, at((quarter ^ k) * 32, 32), :] = ref[:, 128:160, :]
        for k, ref in enumerate((mid0, mid1)):
            h = half ^ k
            for n in (0, 1):
                b_s[:, rel(h * 2 + n), :] = ref[:, n * 128 : n * 128 + 128, :]
            am_s[:, at(h * 64, 64), :] = ref[:, 256:320, :]
            d_s[:, at(h * 64, 64), :] = ref[:, 320:384, :]
        masks = [mask_ref[r : r + 1, :] for r in range(4)]

        def put_x(j, r, re, im):
            put_rhs(x_h.at[j], x_l.at[j], r * 256, re, im)

        put_rhs(ra_h, ra_l, 0, am_s[0], am_s[1])
        for r in range(4):
            rows = slice(r * 128, r * 128 + 128)
            re, im = l_s[0, rows] * masks[r], l_s[1, rows] * masks[r]
            put_pair(lhs_h, lhs_l, r * 128, 256, re, im)
            put_x(0, r, re, im)
            put_transposed(tt_h, tt_l, 0, r, re, im)
        put_pair(lhs_h, lhs_l, 640, 256, t0_s[0], t0_s[1])
        ah, al = ra_h[...], ra_l[...]
        got = mm3(lhs_h[0:512, 256:512], lhs_l[0:512, 256:512], ah, al)
        for r in range(4):
            rows = slice(r * 128, r * 128 + 128)
            re = b_s[0, rows] * masks[r] - got[rows, 0:128]
            im = b_s[1, rows] * masks[r] - got[rows, 128:256]
            put_pair(lhs_h, lhs_l, r * 128, 0, re, im)
            put_x(1, r, re, im)
            put_transposed(tt_h, tt_l, 256, r, re, im)
        got = mm3(lhs_h[640:768, 256:512], lhs_l[640:768, 256:512], ah, al)
        q_r, q_i = -got[:, 0:128], -got[:, 128:256]
        put_pair(lhs_h, lhs_l, 640, 0, q_r, q_i)
        put_pair(lhs_h, lhs_l, 512, 256, q_r.T, q_i.T)
        put_rhs(rq_h, rq_l, 0, q_r, q_i)
        put_pair(aux_h, aux_l, 0, 0, am_s[0].T, am_s[1].T)
        got = mm3(aux_h[...], aux_l[...], rq_h[...], rq_l[...])
        d_r, d_i = d_s[0] - got[:, 0:128], d_s[1] - got[:, 128:256]
        put_pair(lhs_h, lhs_l, 512, 0, d_r, d_i)
        base_top[0] = t0_s[...]
        base_top[1, 0] = q_r
        base_top[1, 1] = q_i
        base_top[2, 0] = d_r
        base_top[2, 1] = d_i

        for copy in links:
            copy.wait()
        for j in range(leaves):
            mine = slice(j * 128, j * 128 + 128)
            put_rhs(rhs_h.at[j], rhs_l.at[j], 0, lc_s[0, mine], lc_s[1, mine])
            put_rhs(rhs_h.at[j], rhs_l.at[j], 256, le_s[0, mine], le_s[1, mine])
            put_pair(auxl_h.at[j], auxl_l.at[j], 0, 0, lc_s[0, mine].T, lc_s[1, mine].T)
            put_pair(auxl_h.at[j], auxl_l.at[j], 0, 256, le_s[0, mine].T, le_s[1, mine].T)
        for j in range(leaves):
            panels[j].wait()
            got = mm3(lhs_h[...], lhs_l[...], rhs_h[j], rhs_l[j])
            for r in range(4):
                rows = slice(r * 128, r * 128 + 128)
                mine = at(j * 512 + (plane ^ r) * 128, 128)
                re = g_s[0, mine] * masks[r] - got[rows, 0:128]
                im = g_s[1, mine] * masks[r] - got[rows, 128:256]
                put_x(2 + j, r, re, im)
                put_transposed(tl_h.at[j], tl_l.at[j], 0, r, re, im)
            r_r, r_i = -got[512:640, 0:128], -got[512:640, 128:256]
            s_r, s_i = -got[640:768, 0:128], -got[640:768, 128:256]
            put_rhs(rrs_h.at[j], rrs_l.at[j], 0, r_r, r_i)
            put_rhs(rrs_h.at[j], rrs_l.at[j], 256, s_r, s_i)
            base_leaf[j, 0, 0] = s_r
            base_leaf[j, 0, 1] = s_i
            base_leaf[j, 1, 0] = r_r
            base_leaf[j, 1, 1] = r_i
        copies[-1].wait()
        for j in range(leaves):
            mine = slice(j * 128, j * 128 + 128)
            got = mm3(auxl_h[j], auxl_l[j], rrs_h[j], rrs_l[j])
            base_leaf[j, 2, 0] = li_s[0, mine] - got[:, 0:128]
            base_leaf[j, 2, 1] = li_s[1, mine] - got[:, 128:256]

    return kernel


def front(planes, masks, tops, mids, panel_leaf, link_c, link_e, inv_leaf):
    leaves = panel_leaf.shape[1] // 512
    n = leaves + 2
    v = pltpu.VMEM
    out = [
        ((n, 1024, 256), BF16), ((n, 1024, 256), BF16), ((512, 512), BF16), ((512, 512), BF16),
        ((leaves, 256, 512), BF16), ((leaves, 256, 512), BF16),
        ((3, 2, 128, 128), F32), ((leaves, 3, 2, 128, 128), F32),
    ]
    pair = lambda *shape: [v(shape, BF16)] * 2
    return pl.pallas_call(
        make_front_kernel(planes, leaves),
        out_shape=tuple(jax.ShapeDtypeStruct(s, d) for s, d in out),
        in_specs=[VMEM] * 7 + [ANY] * 4,
        out_specs=(VMEM,) * len(out),
        scratch_shapes=[
            v((2, 512, 128), F32), v((2, 512, 128), F32),
            v((2, 128, 128), F32), v((2, 128, 128), F32), v((2, 128, 128), F32),
            v((2, leaves * 512, 128), F32),
            v((2, leaves * 128, 128), F32), v((2, leaves * 128, 128), F32), v((2, leaves * 128, 128), F32),
            *pair(768, 512), *pair(256, 256), *pair(256, 256), *pair(128, 256),
            *pair(leaves, 512, 256), *pair(leaves, 512, 256), *pair(leaves, 128, 512),
            pltpu.SemaphoreType.DMA((3 + leaves,)),
        ],
        compiler_params=pltpu.CompilerParams(vmem_limit_bytes=24 << 20),
        cost_estimate=pl.CostEstimate(flops=1_000_000, bytes_accessed=1_000, transcendentals=0),
        name="front",
    )(masks, *tops, *mids, in_hbm(panel_leaf), in_hbm(link_c), in_hbm(link_e), in_hbm(inv_leaf))


def make_back_kernel(planes, leaves):
    def kernel(
        mask_ref, a0, a1, a2, a3, z1a, z1b, z2a, z2b, z3a, z3b,
        x_h, x_l, tt_h, tt_l, tl_h, tl_l, base_top, base_leaf,
        col_top, diag_top, col_mid, cross_mid, diag_mid, col_leaf, cross_c, cross_e, diag_leaf,
        own, a_h, a_l, cb_h, cb_l, c_s, d_s, e_s, f_s, top_s, mid_s, sem,
    ):
        device = lax.axis_index("row")
        plane = own_plane(device, planes)
        quarter = device % 4
        half = device % 2
        lower = (quarter // 2) ^ half == 0
        copies = []

        def move(src, dst):
            copy = pltpu.make_async_copy(src, dst, sem.at[len(copies)])
            copy.start()
            copies.append(copy)
            return copy

        raw = move(a0, own.at[:, at(quarter * 32, 32), :])
        masks = [-mask_ref[r : r + 1, :] for r in range(4)]
        for row, a_ref, b_ref, cols in ((1, z1a, z1b, (1, 2, 3)), (2, z2a, z2b, (2, 3)), (3, z3a, z3b, (3,))):
            for n, col in enumerate(cols):
                parts = []
                for part in (0, 1):
                    x = a_ref[part, :, n * 128 : n * 128 + 128]
                    y = b_ref[part, :, n * 128 : n * 128 + 128]
                    parts.append(jnp.concatenate([jnp.where(lower, x, y), jnp.where(lower, y, x)], axis=0))
                re, im = parts
                put_pair(a_h, a_l, row * 128, col * 256, re, im)
                if row != col:
                    put_pair(a_h, a_l, col * 128, row * 256, re.T, im.T)
        for k, ref in enumerate((a1, a2, a3)):
            own[:, at((quarter ^ (k + 1)) * 32, 32), :] = ref[...]
        raw.wait()
        for r in range(4):
            cols = at((plane ^ r) * 128, 128)
            re, im = own[0, :, cols], own[1, :, cols]
            put_pair(a_h, a_l, 0, r * 256, re, im)
            if r:
                put_pair(a_h, a_l, r * 128, 0, re.T, im.T)

        def columns(j, out):
            got = mm3(a_h[...], a_l[...], x_h[j], x_l[j])
            for r in range(4):
                rows = slice(r * 128, r * 128 + 128)
                place = at((plane ^ r) * 128, 128)
                for part in (0, 1):
                    lanes = slice(part * 128, part * 128 + 128)
                    c = got[rows, lanes] * masks[r]
                    hi, lo = halves(c)
                    cb_h[j, rows, lanes] = hi
                    cb_l[j, rows, lanes] = lo
                    out[part, place, :] = c

        def against(j, t_h, t_l):
            got = mm3(t_h, t_l, cb_h[j], cb_l[j])
            outs = []
            for n in range(t_h.shape[0] // 256):
                g = got[n * 256 : n * 256 + 256]
                outs.append((g[0:128, 0:128] - g[128:256, 128:256], g[0:128, 128:256] + g[128:256, 0:128]))
            return outs

        def leaf_tail(j):
            th = jnp.concatenate([tt_h[...], tl_h[j]], axis=0)
            tl = jnp.concatenate([tt_l[...], tl_l[j]], axis=0)
            zs = against(2 + j, th, tl)
            for n, (z, out) in enumerate(zip(zs, (e_s, d_s, f_s))):
                for part in (0, 1):
                    out[j, part] = base_leaf[j, n, part] - z[part]
            mine = slice(j * 128, j * 128 + 128)
            move(e_s.at[j], cross_e.at[:, mine, :])
            move(d_s.at[j], cross_c.at[:, mine, :])
            move(f_s.at[j], diag_leaf.at[:, mine, :])

        for j in range(leaves):
            columns(2 + j, c_s.at[2 + j])
            move(c_s.at[2 + j], col_leaf.at[:, j * 512 : j * 512 + 512, :])
        columns(1, c_s.at[1])
        move(c_s.at[1, :, at(half * 256, 256), :], col_mid)
        columns(0, c_s.at[0])
        move(c_s.at[0, :, at(quarter * 128, 128), :], col_top)
        for j in range(leaves):
            leaf_tail(j)
        zs = against(1, tt_h[...], tt_l[...])
        for n in (0, 1):
            for part in (0, 1):
                mid_s[n, part] = base_top[1 + n, part] - zs[n][part]
        move(mid_s.at[0, :, at(half * 64, 64), :], cross_mid)
        move(mid_s.at[1, :, at(half * 64, 64), :], diag_mid)
        (z,) = against(0, tt_h[0:256], tt_l[0:256])
        for part in (0, 1):
            top_s[part] = base_top[0, part] - z[part]
        move(top_s.at[:, at(quarter * 32, 32), :], diag_top)
        for copy in copies[1:]:
            copy.wait()

    return kernel


def back(planes, masks, own, root, firsts, leaves):
    n = leaves + 2
    v = pltpu.VMEM
    shapes = [(2, 128, 128), (2, 32, 128), (2, 256, 128), (2, 64, 128), (2, 64, 128)]
    shapes += [(2, leaves * rows, 128) for rows in (512, 128, 128, 128)]
    pair = lambda *shape: [v(shape, BF16)] * 2
    return pl.pallas_call(
        make_back_kernel(planes, leaves),
        out_shape=tuple(jax.ShapeDtypeStruct(s, F32) for s in shapes),
        in_specs=[VMEM, ANY] + [VMEM] * (9 + len(firsts)),
        out_specs=(ANY,) * len(shapes),
        scratch_shapes=[
            v((2, 128, 512), F32), *pair(512, 1024), *pair(n, 512, 256), v((n, 2, 512, 128), F32),
            v((leaves, 2, 128, 128), F32), v((leaves, 2, 128, 128), F32), v((leaves, 2, 128, 128), F32),
            v((2, 128, 128), F32), v((2, 2, 128, 128), F32),
            pltpu.SemaphoreType.DMA((10 + 4 * leaves,)),
        ],
        compiler_params=pltpu.CompilerParams(vmem_limit_bytes=24 << 20),
        cost_estimate=pl.CostEstimate(flops=8_000_000_000, bytes_accessed=12_000_000, transcendentals=0),
        name="back",
    )(masks, in_hbm(own[0]), *own[1:], *root, *firsts)


def root_gathered(ainv_root):
    device = lax.axis_index("row")
    full = lax.all_gather(ainv_root, "row", axis=1, tiled=True)
    quarter = device % 4
    side = (quarter // 2) ^ (device % 2)
    own = [lax.dynamic_slice_in_dim(full, (quarter ^ k) * 32, 32, 1) for k in range(4)]
    root = []
    for r in (1, 2, 3):
        for k in (0, 1):
            root.append(
                lax.dynamic_slice_in_dim(full[:, :, r * 128 :], r * 128 + (side ^ k) * 64, 64, 1)
            )
    return own, root


def local(
    ainv_root, pattern, panel_top, inv_top, panel_mid, link_mid, inv_mid,
    panel_leaf, link_leaf_mid, link_leaf_top, inv_leaf,
):
    planes = lax.axis_size("row") == 16
    leaves = panel_leaf.shape[1] // 512
    if planes:
        a_other = swap(ainv_root, 1)
        *sent, top, mid, masks = pack(
            pattern, ainv_root, a_other, panel_top, inv_top, panel_mid, link_mid, inv_mid
        )
        got = [swap_by_core(x, 4 * k, 4 * k + 2) for k, x in zip((1, 2, 3), sent)]
        a_far = swap(ainv_root, 2)
        own = [ainv_root, a_other, a_far, swap(a_far, 1)]
    else:
        top = jnp.concatenate([panel_top, inv_top], axis=1)
        mid = jnp.concatenate([panel_mid, link_mid, inv_mid], axis=1)
        node = lax.dynamic_index_in_dim(pattern, lax.axis_index("row") // 4, 0, keepdims=False)
        masks = jnp.broadcast_to(jnp.pad(node.astype(F32), (0, 4))[:, None], (8, 128))
        own, root = root_gathered(ainv_root)
    far = swap(top, 2)
    firsts = front(
        planes, masks, [top, swap(top, 1), far, swap(far, 1)], [mid, swap(mid, 1)],
        panel_leaf, link_leaf_mid, link_leaf_top, inv_leaf,
    )
    if planes:
        got = lax.optimization_barrier(tuple(got) + tuple(firsts))
        firsts = got[3:]
        root = []
        for x in got[:3]:
            root += [x, swap(x, 1)]
    return back(planes, masks, own, root, firsts, leaves)


def solution(mesh):
    split = P("pole", "row", None)
    return jax.shard_map(
        local,
        mesh=mesh,
        in_specs=(split, P()) + (split,) * 9,
        out_specs=(split,) * 9,
        check_vma=False,
    )
```

profile of v0, /device:TPU:0, one launch (start us, length us, event | category | flops | bytes accessed | tf_op | source)
XLA Modules:
  0.0 36.2 jit_solution(13789140863157613034)
XLA Ops:
  0.6 0.5 %collective-permute-start = (f32[2,32,512]{2,1,0:T(8,128)}, f32[2,32,512]{2,1,0:T(8,128)S(1)}, u32[]{:S(2)}, u32[]{:S(2)}) collective-permute-start(f32[2,32,512]{2,1,0:T(8,128)} %a0.1), channel_id=1, source_target_pairs={{0,1},{1,0},{2,3},{3,2},{4,5},{5,4},{6,7},{7,6},{8,9},{9,8},{10,11... | collective-permute-start | bytes 393224 | tf_op jit(solution)/shard_map/ppermute | solution.py:15
  1.2 1.2 %collective-permute-done.a_other.a1 = f32[2,32,512]{2,1,0:T(8,128)S(1)} collective-permute-done((f32[2,32,512]{2,1,0:T(8,128)}, f32[2,32,512]{2,1,0:T(8,128)S(1)}, u32[]{:S(2)}, u32[]{:S(2)}) %collective-permute-start) | collective-permute-done | bytes 131104 | tf_op jit(solution)/shard_map/ppermute | solution.py:15
  2.4 1.2 %pack_sent.1 = (f32[2,64,384]{2,1,0:T(8,128)S(1)}, f32[2,64,256]{2,1,0:T(8,128)S(1)}, f32[2,64,128]{2,1,0:T(8,128)S(1)}, f32[2,160,128]{2,1,0:T(8,128)S(1)}, f32...) custom-call(s32[4,4]{1,0:T(4,128)} %pat.1, f32[2,32,512]{2,1,0:T(8,128)} %a0.1, ...), custom_call_target="tpu_custom_call" | custom-call | tf_op jit(solution)/shard_map/pack_sent/pallas_call | solution.py:92
  3.5 0.4 %collective-permute-start.9 = (f32[2,384,128]{2,1,0:T(8,128)S(1)}, f32[2,384,128]{2,1,0:T(8,128)S(1)}, u32[]{:S(2)}, u32[]{:S(2)}) collective-permute-start(f32[2,384,128]{2,1,0:T(8,128)S(1)} %get-tuple-element.39.mid0), channel_id=1, source_target_pairs={{0,1},{1,0},{2,3},{3,2},{4,5},{5,4},{6,7},{7,6},{8,9},{9,8},{10,11... | collective-permute-start | bytes 1179656 | tf_op jit(solution)/shard_map/ppermute | solution.py:15
  4.0 2.7 %collective-permute-start.7 = (f32[2,160,128]{2,1,0:T(8,128)S(1)}, f32[2,160,128]{2,1,0:T(8,128)S(1)}, u32[]{:S(2)}, u32[]{:S(2)}) collective-permute-start(f32[2,160,128]{2,1,0:T(8,128)S(1)} %get-tuple-element.38.top0), channel_id=1, source_target_pairs={{0,2},{1,3},{2,0},{3,1},{4,6},{5,7},{6,4},{7,5},{8,10},{9,11},{10,... | collective-permute-start | bytes 491528 | tf_op jit(solution)/shard_map/ppermute | solution.py:15
  6.6 0.1 collective-permute-start.6
  6.7 4.6 %collective-permute-done.7.top2 = f32[2,160,128]{2,1,0:T(8,128)S(1)} collective-permute-done((f32[2,160,128]{2,1,0:T(8,128)S(1)}, f32[2,160,128]{2,1,0:T(8,128)S(1)}, u32[]{:S(2)}, u32[]{:S(2)}) %collective-permute-start.7) | collective-permute-done | bytes 163872 | tf_op jit(solution)/shard_map/ppermute | solution.py:15
  11.4 1.8 %collective-permute-start.3 = (f32[2,64,384]{2,1,0:T(8,128)S(1)}, f32[2,64,384]{2,1,0:T(8,128)S(1)}, u32[]{:S(2)}, u32[]{:S(2)}) collective-permute-start(f32[2,64,384]{2,1,0:T(8,128)S(1)} %get-tuple-element.35), channel_id=1, source_target_pairs={{0,4},{1,7},{2,6},{3,5},{4,0},{5,3},{6,2},{7,1},{8,12},{9,15},{10,... | collective-permute-start | bytes 589832 | tf_op jit(solution)/shard_map/ppermute | solution.py:19
  13.2 2.6 %collective-permute-start.4 = (f32[2,64,256]{2,1,0:T(8,128)S(1)}, f32[2,64,256]{2,1,0:T(8,128)S(1)}, u32[]{:S(2)}, u32[]{:S(2)}) collective-permute-start(f32[2,64,256]{2,1,0:T(8,128)S(1)} %get-tuple-element.36), channel_id=1, source_target_pairs={{0,8},{1,11},{2,10},{3,9},{4,12},{5,15},{6,14},{7,13},{8,0},{9,3},... | collective-permute-start | bytes 393224 | tf_op jit(solution)/shard_map/ppermute | solution.py:19
  15.8 1.7 %collective-permute-start.1 = (f32[2,32,512]{2,1,0:T(8,128)}, f32[2,32,512]{2,1,0:T(8,128)S(1)}, u32[]{:S(2)}, u32[]{:S(2)}) collective-permute-start(f32[2,32,512]{2,1,0:T(8,128)} %a0.1), channel_id=1, source_target_pairs={{0,2},{1,3},{2,0},{3,1},{4,6},{5,7},{6,4},{7,5},{8,10},{9,11},{10,... | collective-permute-start | bytes 393224 | tf_op jit(solution)/shard_map/ppermute | solution.py:15
  17.5 0.0 collective-permute-done.9.mid1
  17.5 7.4 %front.1 = (bf16[5,1024,256]{2,1,0:T(8,128)(2,1)S(1)}, bf16[5,1024,256]{2,1,0:T(8,128)(2,1)S(1)}, bf16[512,512]{1,0:T(8,128)(2,1)S(1)}, bf16[512,512]{1,0:T(8,12...) custom-call(f32[8,128]{1,0:T(8,128)S(1)} %get-tuple-element.34.mask_, ...), custom_call_target="tpu_custom_call" | custom-call | flops 1000000 | bytes 1000 | tf_op jit(solution)/shard_map/front/pallas_call | solution.py:246
  24.9 0.4 %collective-permute-done.5.z3a = f32[2,64,128]{2,1,0:T(8,128)S(1)} collective-permute-done((f32[2,64,128]{2,1,0:T(8,128)S(1)}, f32[2,64,128]{2,1,0:T(8,128)S(1)}, u32[]{:S(2)}, u32[]{:S(2)}) %collective-permute-start.5) | collective-permute-done | bytes 65568 | tf_op jit(solution)/shard_map/ppermute | solution.py:19
  25.3 0.0 collective-permute-done.4.z2a
  25.3 0.0 collective-permute-done.3.z1a
  25.3 0.2 collective-permute-start.10
  25.5 0.0 collective-permute-done.1.a2
  25.5 0.3 collective-permute-start.2
  25.8 0.2 collective-permute-start.11
  26.0 0.3 collective-permute-start.12
  26.3 0.6 %collective-permute-done.2.a3 = f32[2,32,512]{2,1,0:T(8,128)S(1)} collective-permute-done((f32[2,32,512]{2,1,0:T(8,128)S(1)}, f32[2,32,512]{2,1,0:T(8,128)S(1)}, u32[]{:S(2)}, u32[]{:S(2)}) %collective-permute-start.2) | collective-permute-done | bytes 131104 | tf_op jit(solution)/shard_map/ppermute | solution.py:15
  26.9 0.4 %collective-permute-done.12.z3b = f32[2,64,128]{2,1,0:T(8,128)S(1)} collective-permute-done((f32[2,64,128]{2,1,0:T(8,128)S(1)}, f32[2,64,128]{2,1,0:T(8,128)S(1)}, u32[]{:S(2)}, u32[]{:S(2)}) %collective-permute-start.12) | collective-permute-done | bytes 65568 | tf_op jit(solution)/shard_map/ppermute | solution.py:15
  27.3 0.0 collective-permute-done.11.z2b
  27.3 8.9 %back.1 = (f32[2,128,128]{2,1,0:T(8,128)}, f32[2,32,128]{2,1,0:T(8,128)}, f32[2,256,128]{2,1,0:T(8,128)}, f32[2,64,128]{2,1,0:T(8,128)}, f32[2,64,128]{2,1,0:T(8...) custom-call(f32[8,128]{1,0:T(8,128)S(1)} %get-tuple-element.34.mask_r, ...), custom_call_target="tpu_custom_call" | custom-call | flops 8000000000 | bytes 12000000 | tf_op jit(solution)/shard_map/back/pallas_call | solution.py:373
  (5 shorter events, 0.0 us)
Async XLA Ops:
  0.6 1.7 %collective-permute-start = (f32[2,32,512]{2,1,0:T(8,128)}, f32[2,32,512]{2,1,0:T(8,128)S(1)}, u32[]{:S(2)}, u32[]{:S(2)}) collective-permute-start(f32[2,32,512]{2,1,0:T(8,128)} %a0.1), channel_id=1, source_target_pairs={{0,1},{1,0},{2,3},{3,2},{4,5},{5,4},{6,7},{7,6},{8,9},{9,8},{10,11... | collective-permute-start | bytes 393224 | tf_op jit(solution)/shard_map/ppermute | solution.py:15
  3.5 14.0 %collective-permute-start.9 = (f32[2,384,128]{2,1,0:T(8,128)S(1)}, f32[2,384,128]{2,1,0:T(8,128)S(1)}, u32[]{:S(2)}, u32[]{:S(2)}) collective-permute-start(f32[2,384,128]{2,1,0:T(8,128)S(1)} %get-tuple-element.39.mid0), channel_id=1, source_target_pairs={{0,1},{1,0},{2,3},{3,2},{4,5},{5,4},{6,7},{7,6},{8,9},{9,8},{10,11... | collective-permute-start | bytes 1179656 | tf_op jit(solution)/shard_map/ppermute | solution.py:15
  4.0 7.4 %collective-permute-start.7 = (f32[2,160,128]{2,1,0:T(8,128)S(1)}, f32[2,160,128]{2,1,0:T(8,128)S(1)}, u32[]{:S(2)}, u32[]{:S(2)}) collective-permute-start(f32[2,160,128]{2,1,0:T(8,128)S(1)} %get-tuple-element.38.top0), channel_id=1, source_target_pairs={{0,2},{1,3},{2,0},{3,1},{4,6},{5,7},{6,4},{7,5},{8,10},{9,11},{10,... | collective-permute-start | bytes 491528 | tf_op jit(solution)/shard_map/ppermute | solution.py:15
  6.6 9.1 %collective-permute-start.6 = (f32[2,160,128]{2,1,0:T(8,128)S(1)}, f32[2,160,128]{2,1,0:T(8,128)S(1)}, u32[]{:S(2)}, u32[]{:S(2)}) collective-permute-start(f32[2,160,128]{2,1,0:T(8,128)S(1)} %get-tuple-element.38.top0), channel_id=1, source_target_pairs={{0,1},{1,0},{2,3},{3,2},{4,5},{5,4},{6,7},{7,6},{8,9},{9,8},{10,11... | collective-permute-start | bytes 491528 | tf_op jit(solution)/shard_map/ppermute | solution.py:15
  11.3 4.4 %collective-permute-start.8 = (f32[2,160,128]{2,1,0:T(8,128)S(1)}, f32[2,160,128]{2,1,0:T(8,128)S(1)}, u32[]{:S(2)}, u32[]{:S(2)}) collective-permute-start(f32[2,160,128]{2,1,0:T(8,128)S(1)} %collective-permute-done.7.top2), channel_id=1, source_target_pairs={{0,1},{1,0},{2,3},{3,2},{4,5},{5,4},{6,7},{7,6},{8,9},{9,8},{10,11... | collective-permute-start | bytes 491528 | tf_op jit(solution)/shard_map/ppermute | solution.py:15
  11.4 13.9 %collective-permute-start.3 = (f32[2,64,384]{2,1,0:T(8,128)S(1)}, f32[2,64,384]{2,1,0:T(8,128)S(1)}, u32[]{:S(2)}, u32[]{:S(2)}) collective-permute-start(f32[2,64,384]{2,1,0:T(8,128)S(1)} %get-tuple-element.35), channel_id=1, source_target_pairs={{0,4},{1,7},{2,6},{3,5},{4,0},{5,3},{6,2},{7,1},{8,12},{9,15},{10,... | collective-permute-start | bytes 589832 | tf_op jit(solution)/shard_map/ppermute | solution.py:19
  13.2 12.1 %collective-permute-start.4 = (f32[2,64,256]{2,1,0:T(8,128)S(1)}, f32[2,64,256]{2,1,0:T(8,128)S(1)}, u32[]{:S(2)}, u32[]{:S(2)}) collective-permute-start(f32[2,64,256]{2,1,0:T(8,128)S(1)} %get-tuple-element.36), channel_id=1, source_target_pairs={{0,8},{1,11},{2,10},{3,9},{4,12},{5,15},{6,14},{7,13},{8,0},{9,3},... | collective-permute-start | bytes 393224 | tf_op jit(solution)/shard_map/ppermute | solution.py:19
  15.7 9.5 %collective-permute-start.5 = (f32[2,64,128]{2,1,0:T(8,128)S(1)}, f32[2,64,128]{2,1,0:T(8,128)S(1)}, u32[]{:S(2)}, u32[]{:S(2)}) collective-permute-start(f32[2,64,128]{2,1,0:T(8,128)S(1)} %get-tuple-element.37), channel_id=1, source_target_pairs={{0,12},{1,15},{2,14},{3,13},{4,8},{5,11},{6,10},{7,9},{8,4},{9,7},... | collective-permute-start | bytes 196616 | tf_op jit(solution)/shard_map/ppermute | solution.py:19
  15.8 9.8 %collective-permute-start.1 = (f32[2,32,512]{2,1,0:T(8,128)}, f32[2,32,512]{2,1,0:T(8,128)S(1)}, u32[]{:S(2)}, u32[]{:S(2)}) collective-permute-start(f32[2,32,512]{2,1,0:T(8,128)} %a0.1), channel_id=1, source_target_pairs={{0,2},{1,3},{2,0},{3,1},{4,6},{5,7},{6,4},{7,5},{8,10},{9,11},{10,... | collective-permute-start | bytes 393224 | tf_op jit(solution)/shard_map/ppermute | solution.py:15
  25.3 2.0 %collective-permute-start.10 = (f32[2,64,384]{2,1,0:T(8,128)S(1)}, f32[2,64,384]{2,1,0:T(8,128)S(1)}, u32[]{:S(2)}, u32[]{:S(2)}) collective-permute-start(f32[2,64,384]{2,1,0:T(8,128)S(1)} %collective-permute-done.3.z1a), channel_id=1, source_target_pairs={{0,1},{1,0},{2,3},{3,2},{4,5},{5,4},{6,7},{7,6},{8,9},{9,8},{10,11... | collective-permute-start | bytes 589832 | tf_op jit(solution)/shard_map/ppermute | solution.py:15
  25.5 1.4 %collective-permute-start.2 = (f32[2,32,512]{2,1,0:T(8,128)S(1)}, f32[2,32,512]{2,1,0:T(8,128)S(1)}, u32[]{:S(2)}, u32[]{:S(2)}) collective-permute-start(f32[2,32,512]{2,1,0:T(8,128)S(1)} %collective-permute-done.1.a2), channel_id=1, source_target_pairs={{0,1},{1,0},{2,3},{3,2},{4,5},{5,4},{6,7},{7,6},{8,9},{9,8},{10,11... | collective-permute-start | bytes 393224 | tf_op jit(solution)/shard_map/ppermute | solution.py:15
  25.8 1.5 %collective-permute-start.11 = (f32[2,64,256]{2,1,0:T(8,128)S(1)}, f32[2,64,256]{2,1,0:T(8,128)S(1)}, u32[]{:S(2)}, u32[]{:S(2)}) collective-permute-start(f32[2,64,256]{2,1,0:T(8,128)S(1)} %collective-permute-done.4.z2a), channel_id=1, source_target_pairs={{0,1},{1,0},{2,3},{3,2},{4,5},{5,4},{6,7},{7,6},{8,9},{9,8},{10,11... | collective-permute-start | bytes 393224 | tf_op jit(solution)/shard_map/ppermute | solution.py:15
  26.0 1.3 %collective-permute-start.12 = (f32[2,64,128]{2,1,0:T(8,128)S(1)}, f32[2,64,128]{2,1,0:T(8,128)S(1)}, u32[]{:S(2)}, u32[]{:S(2)}) collective-permute-start(f32[2,64,128]{2,1,0:T(8,128)S(1)} %collective-permute-done.5.z3a), channel_id=1, source_target_pairs={{0,1},{1,0},{2,3},{3,2},{4,5},{5,4},{6,7},{7,6},{8,9},{9,8},{10,11... | collective-permute-start | bytes 196616 | tf_op jit(solution)/shard_map/ppermute | solution.py:15
where the time goes:
time: 36.4 us; the launch traced here: 36.2 us
  Pallas kernels  17.5 us (48%)
  starting transfers between devices  10.8 us (30%)
  waiting for transfers between devices  7.21 us (20%)
  between operations  0.68 us (2%)
    pallas_call x1, Pallas kernels, back(): pl.pallas_call(make_back_kernel(planes, leaves), out_shape=tuple((jax.Sha...  8.9 us
    pallas_call x1, Pallas kernels, front(): pl.pallas_call(make_front_kernel(planes, leaves), out_shape=tuple((jax.Sh...  7.39 us
    ppermute x10, waiting for transfers between devices, swap(): lax.ppermute(x, 'row', [(i, i ^ apart) for i in range(lax.axis_size('row'...  6.82 us
    ppermute x10, starting transfers between devices, swap(): lax.ppermute(x, 'row', [(i, i ^ apart) for i in range(lax.axis_size('row'...  6.45 us
    ppermute x3, starting transfers between devices, swap_by_core(): lax.ppermute(x, 'row', [(i, i ^ (apart_odd if i & 1 else apart_even)) for...  4.39 us
    pallas_call x1, Pallas kernels, pack(): pl.pallas_call(pack_kernel, out_shape=tuple((jax.ShapeDtypeStruct(s, F32)...  1.16 us
  transfers between devices with their start and end apart: 13, of which 5 were waited for; matrix products, arithmetic and copies ran while one was open for 0% of the time, Pallas kernels for 20%

commit v1 on v0

v1 whole, which is shorter than its diff:
```python
import jax
import jax.numpy as jnp
from jax import lax
from jax.experimental import pallas as pl
from jax.experimental.pallas import tpu as pltpu
from jax.sharding import PartitionSpec as P

F32 = jnp.float32
BF16 = jnp.bfloat16
ANY = pl.BlockSpec(memory_space=pl.ANY)
VMEM = pl.BlockSpec(memory_space=pltpu.VMEM)


def swap(x, apart):
    return lax.ppermute(x, "row", [(i, i ^ apart) for i in range(lax.axis_size("row"))])


def halves(x):
    hi = x.astype(BF16)
    return hi, (x - hi.astype(F32)).astype(BF16)


def mm(a, b):
    return jnp.dot(a, b, preferred_element_type=F32)


def mm3(ah, al, bh, bl):
    return mm(ah, bh) + (mm(ah, bl) + mm(al, bh))


def at(start, size):
    return pl.ds(pl.multiple_of(start, size), size)


def in_hbm(x):
    return pltpu.with_memory_space_constraint(x, pltpu.HBM)


def own_plane(device, planes):
    return device // 4 if planes else device * 0


def pack_kernel(pat, a_hbm, t_hbm, i_hbm, pm_hbm, lm_hbm, im_hbm, top, mid, masks, z1, z2, z3, pat_s, sem):
    plane = lax.axis_index("row") // 4
    pairs = [
        (pat, pat_s),
        (t_hbm, top.at[:, 0:128, :]), (i_hbm, top.at[:, 128:160, :]),
        (pm_hbm, mid.at[:, 0:256, :]), (lm_hbm, mid.at[:, 256:320, :]), (im_hbm, mid.at[:, 320:384, :]),
    ]
    for n in range(4):
        pairs.append((a_hbm.at[:, :, n * 128 : n * 128 + 128], top.at[:, 160 + n * 32 : 192 + n * 32, :]))
    for dst, order in ((z1, (0, 3, 2)), (z2, (0, 1)), (z3, (0,))):
        for n, apart in enumerate(order):
            pairs.append((a_hbm.at[:, :, at((plane ^ apart) * 128, 128)], dst.at[:, n * 32 : n * 32 + 32, :]))
    copies = [pltpu.make_async_copy(src, dst, sem.at[n]) for n, (src, dst) in enumerate(pairs)]
    for copy in copies:
        copy.start()
    copies[0].wait()
    for r in range(4):
        masks[r : r + 1, :] = jnp.full((1, 128), pat_s[plane, plane ^ r], jnp.int32).astype(F32)
    masks[4:8, :] = jnp.zeros((4, 128), F32)
    for copy in copies[1:]:
        copy.wait()


def pack(pattern, *mine):
    shapes = [(2, 288, 128), (2, 384, 128), (8, 128), (2, 96, 128), (2, 64, 128), (2, 32, 128)]
    return pl.pallas_call(
        pack_kernel,
        out_shape=tuple(jax.ShapeDtypeStruct(s, F32) for s in shapes),
        in_specs=[ANY] * 7,
        out_specs=(VMEM,) * len(shapes),
        scratch_shapes=[pltpu.SMEM(pattern.shape, jnp.int32), pltpu.SemaphoreType.DMA((16,))],
        compiler_params=pltpu.CompilerParams(vmem_limit_bytes=4 << 20),
        cost_estimate=pl.CostEstimate(flops=1_000_000, bytes_accessed=1_000, transcendentals=0),
        name="pack_panels",
    )(in_hbm(pattern), *(in_hbm(x) for x in mine))


def join_kernel(z1, z2, z3, joined):
    joined[:, 0:96, :] = z1[...]
    joined[:, 96:160, :] = z2[...]
    joined[:, 160:192, :] = z3[...]


def join(*blocks):
    return pl.pallas_call(
        join_kernel,
        out_shape=jax.ShapeDtypeStruct((2, 192, 128), F32),
        in_specs=[VMEM] * 3,
        out_specs=VMEM,
        compiler_params=pltpu.CompilerParams(vmem_limit_bytes=4 << 20),
        cost_estimate=pl.CostEstimate(flops=1_000_000, bytes_accessed=1_000, transcendentals=0),
        name="join_root",
    )(*blocks)


def put_rhs(ref_h, ref_l, row, re, im):
    rh, rl = halves(re)
    ih, il = halves(im)
    for ref, r, i in ((ref_h, rh, ih), (ref_l, rl, il)):
        ref[row : row + 128, 0:128] = r
        ref[row : row + 128, 128:256] = i
        ref[row + 128 : row + 256, 0:128] = -i
        ref[row + 128 : row + 256, 128:256] = r


def put_pair(ref_h, ref_l, row, col, re, im):
    n = re.shape[0]
    rh, rl = halves(re)
    ih, il = halves(im)
    for ref, r, i in ((ref_h, rh, ih), (ref_l, rl, il)):
        ref[row : row + n, col : col + 128] = r
        ref[row : row + n, col + 128 : col + 256] = i


def put_transposed(ref_h, ref_l, row, r, re, im):
    for part, x in ((0, re), (128, im)):
        xh, xl = halves(x.T)
        ref_h[row + part : row + part + 128, r * 128 : r * 128 + 128] = xh
        ref_l[row + part : row + part + 128, r * 128 : r * 128 + 128] = xl


def make_prep_kernel(leaves):
    def kernel(panel, link_c, link_e, inv, g, li, rhs_h, rhs_l, auxl_h, auxl_l, lc_s, le_s, sem):
        pairs = ((link_c, lc_s), (link_e, le_s), (panel, g), (inv, li))
        copies = [pltpu.make_async_copy(src, dst, sem.at[n]) for n, (src, dst) in enumerate(pairs)]
        for copy in copies:
            copy.start()
        for row, ref, copy in ((0, lc_s, copies[0]), (256, le_s, copies[1])):
            copy.wait()
            for j in range(leaves):
                mine = slice(j * 128, j * 128 + 128)
                re, im = ref[0, mine], ref[1, mine]
                put_rhs(rhs_h.at[j], rhs_l.at[j], row, re, im)
                put_pair(auxl_h.at[j], auxl_l.at[j], 0, row, re.T, im.T)
        copies[2].wait()
        copies[3].wait()

    return kernel


def prep(panel, link_c, link_e, inv):
    leaves = panel.shape[1] // 512
    v = pltpu.VMEM
    out = [(panel.shape, F32), (inv.shape, F32)]
    out += [((leaves, 512, 256), BF16)] * 2 + [((leaves, 128, 512), BF16)] * 2
    return pl.pallas_call(
        make_prep_kernel(leaves),
        out_shape=tuple(jax.ShapeDtypeStruct(s, d) for s, d in out),
        in_specs=[ANY] * 4,
        out_specs=(VMEM,) * len(out),
        scratch_shapes=[v(link_c.shape, F32), v(link_e.shape, F32), pltpu.SemaphoreType.DMA((4,))],
        compiler_params=pltpu.CompilerParams(vmem_limit_bytes=12 << 20),
        cost_estimate=pl.CostEstimate(flops=1_000_000, bytes_accessed=1_000, transcendentals=0),
        name="prep",
    )(in_hbm(panel), in_hbm(link_c), in_hbm(link_e), in_hbm(inv))


def make_front_kernel(planes, leaves):
    def kernel(
        mask_ref, top0, top1, top2, top3, mid0, mid1, g_s, li_s, rhs_h, rhs_l, auxl_h, auxl_l,
        x_h, x_l, tt_h, tt_l, tl_h, tl_l, base_top, base_leaf, c_own,
        l_s, b_s, t0_s, am_s, d_s, own, row_h, row_l, col_h, col_l,
        lhs_h, lhs_l, ra_h, ra_l, rq_h, rq_l, aux_h, aux_l, rrs_h, rrs_l,
    ):
        device = lax.axis_index("row")
        plane = own_plane(device, planes)
        quarter = device % 4
        half = device % 2
        def rel(supernode):
            return at((supernode ^ plane) * 128, 128)

        for k, ref in enumerate((top0, top1, top2, top3)):
            q = quarter ^ k
            l_s[:, rel(q), :] = ref[:, 0:128, :]
            t0_s[:, at(q * 32, 32), :] = ref[:, 128:160, :]
            for n in range(4):
                own[:, at(q * 32, 32), n * 128 : n * 128 + 128] = ref[:, 160 + n * 32 : 192 + n * 32, :]
        for k, ref in enumerate((mid0, mid1)):
            h = half ^ k
            for n in (0, 1):
                b_s[:, rel(h * 2 + n), :] = ref[:, n * 128 : n * 128 + 128, :]
            am_s[:, at(h * 64, 64), :] = ref[:, 256:320, :]
            d_s[:, at(h * 64, 64), :] = ref[:, 320:384, :]
        masks = [mask_ref[r : r + 1, :] for r in range(4)]

        def put_x(j, r, re, im):
            put_rhs(x_h.at[j], x_l.at[j], r * 256, re, im)

        for r in range(4):
            cols = at((plane ^ r) * 128, 128)
            re, im = own[0, :, cols], own[1, :, cols]
            put_pair(row_h, row_l, 0, r * 256, re, im)
            if r:
                put_pair(col_h, col_l, (r - 1) * 128, 0, re.T, im.T)

        def own_product(j):
            c_own[j, 0:128] = mm3(row_h[...], row_l[...], x_h[j], x_l[j])
            c_own[j, 128:512] = mm3(col_h[...], col_l[...], x_h[j, 0:256], x_l[j, 0:256])

        put_rhs(ra_h, ra_l, 0, am_s[0], am_s[1])
        for r in range(4):
            rows = slice(r * 128, r * 128 + 128)
            re, im = l_s[0, rows] * masks[r], l_s[1, rows] * masks[r]
            put_pair(lhs_h, lhs_l, r * 128, 256, re, im)
            put_x(0, r, re, im)
            put_transposed(tt_h, tt_l, 0, r, re, im)
        put_pair(lhs_h, lhs_l, 640, 256, t0_s[0], t0_s[1])
        ah, al = ra_h[...], ra_l[...]
        got = mm3(lhs_h[0:512, 256:512], lhs_l[0:512, 256:512], ah, al)
        for r in range(4):
            rows = slice(r * 128, r * 128 + 128)
            re = b_s[0, rows] * masks[r] - got[rows, 0:128]
            im = b_s[1, rows] * masks[r] - got[rows, 128:256]
            put_pair(lhs_h, lhs_l, r * 128, 0, re, im)
            put_x(1, r, re, im)
            put_transposed(tt_h, tt_l, 256, r, re, im)
        got = mm3(lhs_h[640:768, 256:512], lhs_l[640:768, 256:512], ah, al)
        q_r, q_i = -got[:, 0:128], -got[:, 128:256]
        put_pair(lhs_h, lhs_l, 640, 0, q_r, q_i)
        put_pair(lhs_h, lhs_l, 512, 256, q_r.T, q_i.T)
        put_rhs(rq_h, rq_l, 0, q_r, q_i)
        put_pair(aux_h, aux_l, 0, 0, am_s[0].T, am_s[1].T)
        got = mm3(aux_h[...], aux_l[...], rq_h[...], rq_l[...])
        d_r, d_i = d_s[0] - got[:, 0:128], d_s[1] - got[:, 128:256]
        put_pair(lhs_h, lhs_l, 512, 0, d_r, d_i)
        base_top[0] = t0_s[...]
        base_top[1, 0] = q_r
        base_top[1, 1] = q_i
        base_top[2, 0] = d_r
        base_top[2, 1] = d_i

        own_product(0)
        own_product(1)
        for j in range(leaves):
            got = mm3(lhs_h[...], lhs_l[...], rhs_h[j], rhs_l[j])
            for r in range(4):
                rows = slice(r * 128, r * 128 + 128)
                mine = at(j * 512 + (plane ^ r) * 128, 128)
                re = g_s[0, mine] * masks[r] - got[rows, 0:128]
                im = g_s[1, mine] * masks[r] - got[rows, 128:256]
                put_x(2 + j, r, re, im)
                put_transposed(tl_h.at[j], tl_l.at[j], 0, r, re, im)
            r_r, r_i = -got[512:640, 0:128], -got[512:640, 128:256]
            s_r, s_i = -got[640:768, 0:128], -got[640:768, 128:256]
            put_rhs(rrs_h.at[j], rrs_l.at[j], 0, r_r, r_i)
            put_rhs(rrs_h.at[j], rrs_l.at[j], 256, s_r, s_i)
            base_leaf[j, 0, 0] = s_r
            base_leaf[j, 0, 1] = s_i
            base_leaf[j, 1, 0] = r_r
            base_leaf[j, 1, 1] = r_i
        for j in range(leaves):
            mine = slice(j * 128, j * 128 + 128)
            got = mm3(auxl_h[j], auxl_l[j], rrs_h[j], rrs_l[j])
            base_leaf[j, 2, 0] = li_s[0, mine] - got[:, 0:128]
            base_leaf[j, 2, 1] = li_s[1, mine] - got[:, 128:256]
            own_product(2 + j)

    return kernel


def front(planes, masks, tops, mids, prepared):
    leaves = prepared[0].shape[1] // 512
    n = leaves + 2
    v = pltpu.VMEM
    out = [
        ((n, 1024, 256), BF16), ((n, 1024, 256), BF16), ((512, 512), BF16), ((512, 512), BF16),
        ((leaves, 256, 512), BF16), ((leaves, 256, 512), BF16),
        ((3, 2, 128, 128), F32), ((leaves, 3, 2, 128, 128), F32), ((n, 512, 256), F32),
    ]
    pair = lambda *shape: [v(shape, BF16)] * 2
    return pl.pallas_call(
        make_front_kernel(planes, leaves),
        out_shape=tuple(jax.ShapeDtypeStruct(s, d) for s, d in out),
        in_specs=[VMEM] * 13,
        out_specs=(VMEM,) * len(out),
        scratch_shapes=[
            v((2, 512, 128), F32), v((2, 512, 128), F32),
            v((2, 128, 128), F32), v((2, 128, 128), F32), v((2, 128, 128), F32),
            v((2, 128, 512), F32), *pair(128, 1024), *pair(384, 256),
            *pair(768, 512), *pair(256, 256), *pair(256, 256), *pair(128, 256),
            *pair(leaves, 512, 256),
        ],
        compiler_params=pltpu.CompilerParams(vmem_limit_bytes=24 << 20),
        cost_estimate=pl.CostEstimate(flops=1_000_000, bytes_accessed=1_000, transcendentals=0),
        name="front",
    )(masks, *tops, *mids, *prepared)


def make_back_kernel(planes, leaves):
    def kernel(
        mask_ref, b0, b1, b2, b3,
        x_h, x_l, tt_h, tt_l, tl_h, tl_l, base_top, base_leaf, c_own,
        col_top, diag_top, col_mid, cross_mid, diag_mid, col_leaf, cross_c, cross_e, diag_leaf,
        blocks, a_h, a_l, cb_h, cb_l, c_s, d_s, e_s, f_s, top_s, mid_s, sem,
    ):
        device = lax.axis_index("row")
        plane = own_plane(device, planes)
        quarter = device % 4
        half = device % 2
        copies = []

        def move(src, dst):
            copy = pltpu.make_async_copy(src, dst, sem.at[len(copies)])
            copy.start()
            copies.append(copy)
            return copy

        masks = [-mask_ref[r : r + 1, :] for r in range(4)]
        for k, ref in enumerate((b0, b1, b2, b3)):
            for n in range(6):
                blocks[n, :, at((quarter ^ k) * 32, 32), :] = ref[:, n * 32 : n * 32 + 32, :]
        for n, (row, col) in enumerate(((1, 1), (1, 2), (1, 3), (2, 2), (2, 3), (3, 3))):
            re, im = blocks[n, 0], blocks[n, 1]
            put_pair(a_h, a_l, row * 128 - 128, col * 256 - 256, re, im)
            if row != col:
                put_pair(a_h, a_l, col * 128 - 128, row * 256 - 256, re.T, im.T)

        def columns(j, out):
            got = mm3(a_h[...], a_l[...], x_h[j, 256:1024], x_l[j, 256:1024])
            for r in range(4):
                rows = slice(r * 128, r * 128 + 128)
                place = at((plane ^ r) * 128, 128)
                for part in (0, 1):
                    lanes = slice(part * 128, part * 128 + 128)
                    c = c_own[j, rows, lanes]
                    if r:
                        c = c + got[r * 128 - 128 : r * 128, lanes]
                    c = c * masks[r]
                    hi, lo = halves(c)
                    cb_h[j, rows, lanes] = hi
                    cb_l[j, rows, lanes] = lo
                    out[part, place, :] = c

        def against(j, t_h, t_l):
            got = mm3(t_h, t_l, cb_h[j], cb_l[j])
            outs = []
            for n in range(t_h.shape[0] // 256):
                g = got[n * 256 : n * 256 + 256]
                outs.append((g[0:128, 0:128] - g[128:256, 128:256], g[0:128, 128:256] + g[128:256, 0:128]))
            return outs

        def leaf_tail(j):
            th = jnp.concatenate([tt_h[...], tl_h[j]], axis=0)
            tl = jnp.concatenate([tt_l[...], tl_l[j]], axis=0)
            zs = against(2 + j, th, tl)
            for n, (z, out) in enumerate(zip(zs, (e_s, d_s, f_s))):
                for part in (0, 1):
                    out[j, part] = base_leaf[j, n, part] - z[part]
            mine = slice(j * 128, j * 128 + 128)
            move(e_s.at[j], cross_e.at[:, mine, :])
            move(d_s.at[j], cross_c.at[:, mine, :])
            move(f_s.at[j], diag_leaf.at[:, mine, :])

        for j in range(leaves):
            columns(2 + j, c_s.at[2 + j])
            move(c_s.at[2 + j], col_leaf.at[:, j * 512 : j * 512 + 512, :])
        columns(1, c_s.at[1])
        move(c_s.at[1, :, at(half * 256, 256), :], col_mid)
        columns(0, c_s.at[0])
        move(c_s.at[0, :, at(quarter * 128, 128), :], col_top)
        for j in range(leaves):
            leaf_tail(j)
        zs = against(1, tt_h[...], tt_l[...])
        for n in (0, 1):
            for part in (0, 1):
                mid_s[n, part] = base_top[1 + n, part] - zs[n][part]
        move(mid_s.at[0, :, at(half * 64, 64), :], cross_mid)
        move(mid_s.at[1, :, at(half * 64, 64), :], diag_mid)
        (z,) = against(0, tt_h[0:256], tt_l[0:256])
        for part in (0, 1):
            top_s[part] = base_top[0, part] - z[part]
        move(top_s.at[:, at(quarter * 32, 32), :], diag_top)
        for copy in copies:
            copy.wait()

    return kernel


def back(planes, masks, root, firsts, leaves):
    n = leaves + 2
    v = pltpu.VMEM
    shapes = [(2, 128, 128), (2, 32, 128), (2, 256, 128), (2, 64, 128), (2, 64, 128)]
    shapes += [(2, leaves * rows, 128) for rows in (512, 128, 128, 128)]
    pair = lambda *shape: [v(shape, BF16)] * 2
    return pl.pallas_call(
        make_back_kernel(planes, leaves),
        out_shape=tuple(jax.ShapeDtypeStruct(s, F32) for s in shapes),
        in_specs=[VMEM] * (5 + len(firsts)),
        out_specs=(ANY,) * len(shapes),
        scratch_shapes=[
            v((6, 2, 128, 128), F32), *pair(384, 768), *pair(n, 512, 256), v((n, 2, 512, 128), F32),
            v((leaves, 2, 128, 128), F32), v((leaves, 2, 128, 128), F32), v((leaves, 2, 128, 128), F32),
            v((2, 128, 128), F32), v((2, 2, 128, 128), F32),
            pltpu.SemaphoreType.DMA((10 + 4 * leaves,)),
        ],
        compiler_params=pltpu.CompilerParams(vmem_limit_bytes=24 << 20),
        cost_estimate=pl.CostEstimate(flops=8_000_000_000, bytes_accessed=12_000_000, transcendentals=0),
        name="back",
    )(masks, *root, *firsts)


def root_gathered(ainv_root):
    device = lax.axis_index("row")
    full = lax.all_gather(ainv_root, "row", axis=1, tiled=True)
    quarter = device % 4
    own = lax.dynamic_slice_in_dim(full, quarter * 32, 32, 1)
    root = []
    for k in range(4):
        pieces = []
        for row, col in ((1, 1), (1, 2), (1, 3), (2, 2), (2, 3), (3, 3)):
            block = full[:, row * 128 : row * 128 + 128, col * 128 : col * 128 + 128]
            pieces.append(lax.dynamic_slice_in_dim(block, (quarter ^ k) * 32, 32, 1))
        root.append(jnp.concatenate(pieces, axis=1))
    return own, root


def local(
    ainv_root, pattern, panel_top, inv_top, panel_mid, link_mid, inv_mid,
    panel_leaf, link_leaf_mid, link_leaf_top, inv_leaf,
):
    planes = lax.axis_size("row") == 16
    leaves = panel_leaf.shape[1] // 512
    prepared = prep(panel_leaf, link_leaf_mid, link_leaf_top, inv_leaf)
    if planes:
        top, mid, masks, *sent = pack(
            pattern, ainv_root, panel_top, inv_top, panel_mid, link_mid, inv_mid
        )
        got = [swap(x, 4 * k) for k, x in zip((1, 2, 3), sent)]
        *got, top_1, mid_1 = lax.optimization_barrier((*got, top, mid, *prepared))[:5]
        far_top = swap(top, 2)
        tops = [top, swap(top_1, 1), far_top, swap(far_top, 1)]
        mids = [mid, swap(mid_1, 1)]
        near = join(*got)
        far = swap(near, 2)
        root = [near, swap(near, 1)]
    else:
        mid = jnp.concatenate([panel_mid, link_mid, inv_mid], axis=1)
        node = lax.dynamic_index_in_dim(pattern, lax.axis_index("row") // 4, 0, keepdims=False)
        masks = jnp.broadcast_to(jnp.pad(node.astype(F32), (0, 4))[:, None], (8, 128))
        own, root = root_gathered(ainv_root)
        own = [own[:, :, n * 128 : n * 128 + 128] for n in range(4)]
        top = jnp.concatenate([panel_top, inv_top, *own], axis=1)
        far_top = swap(top, 2)
        tops = [top, swap(top, 1), far_top, swap(far_top, 1)]
        mids = [mid, swap(mid, 1)]
    firsts = front(planes, masks, tops, mids, prepared)
    if planes:
        far, *firsts = lax.optimization_barrier((far, *firsts))
        root += [far, swap(far, 1)]
    return back(planes, masks, root, firsts, leaves)


def solution(mesh):
    split = P("pole", "row", None)
    return jax.shard_map(
        local,
        mesh=mesh,
        in_specs=(split, P()) + (split,) * 9,
        out_specs=(split,) * 9,
        check_vma=False,
    )
```

time: 36.4 us -> 30.6 us (0.84)
  Pallas kernels: 17.5 us -> 14.5 us
  starting transfers between devices: 10.8 us -> 8.93 us
  waiting for transfers between devices: 7.21 us -> 6.27 us
    ppermute x3 -> x0, starting transfers between devices: 4.39 us -> none  [swap_by_core(): lax.ppermute(x, 'row', [(i, i ^ (apart_odd if i & 1 else apart_even)) for...]
    pallas_call x1, Pallas kernels: 8.9 us -> 5.96 us  [back(): pl.pallas_call(make_back_kernel(planes, leaves), out_shape=tuple((jax.Sha...]
    ppermute x10, starting transfers between devices: 6.45 us -> 8.93 us  [swap(): lax.ppermute(x, 'row', [(i, i ^ apart) for i in range(lax.axis_size('row'...]
    pallas_call x1, Pallas kernels: 7.39 us -> 5.57 us  [front(): pl.pallas_call(make_front_kernel(planes, leaves), out_shape=tuple((jax.Sh...]
    pallas_call x0 -> x2, Pallas kernels: none -> 1.75 us  [the longest x1 1.74 us: prep(): pl.pallas_call(make_prep_kernel(leaves), out_shape=tuple((jax.ShapeDtypeS...]
    ppermute x10, waiting for transfers between devices: 6.82 us -> 6.27 us  [swap(): lax.ppermute(x, 'row', [(i, i ^ apart) for i in range(lax.axis_size('row'...]
    ppermute x3 -> x0, waiting for transfers between devices: 0.38 us -> none  [swap_by_core(): lax.ppermute(x, 'row', [(i, i ^ (apart_odd if i & 1 else apart_even)) for...]
  transfers between devices with their start and end apart: 13 -> 10, of which waited for: 5 -> 4; matrix products, arithmetic and copies ran while one was open for 0% -> 0% of each run, Pallas kernels for 20% -> 24%
where the time goes in v1:
time: 30.6 us; the launch traced here: 30.4 us
  Pallas kernels  14.5 us (47%)
  starting transfers between devices  8.93 us (29%)
  waiting for transfers between devices  6.27 us (20%)
  between operations  0.69 us (2%)
    ppermute x10, starting transfers between devices, swap(): lax.ppermute(x, 'row', [(i, i ^ apart) for i in range(lax.axis_size('row'...  8.93 us
    ppermute x10, waiting for transfers between devices, swap(): lax.ppermute(x, 'row', [(i, i ^ apart) for i in range(lax.axis_size('row'...  6.27 us
    pallas_call x1, Pallas kernels, back(): pl.pallas_call(make_back_kernel(planes, leaves), out_shape=tuple((jax.Sha...  5.96 us
    pallas_call x1, Pallas kernels, front(): pl.pallas_call(make_front_kernel(planes, leaves), out_shape=tuple((jax.Sh...  5.57 us
    pallas_call x1, Pallas kernels, prep(): pl.pallas_call(make_prep_kernel(leaves), out_shape=tuple((jax.ShapeDtypeS...  1.74 us
    pallas_call x1, Pallas kernels, pack(): pl.pallas_call(pack_kernel, out_shape=tuple((jax.ShapeDtypeStruct(s, F32)...  1.25 us
  transfers between devices with their start and end apart: 10, of which 4 were waited for; matrix products, arithmetic and copies ran while one was open for 0% of the time, Pallas kernels for 24%

profile of v1, /device:TPU:0, one launch (start us, length us, event | category | flops | bytes accessed | tf_op | source)
XLA Modules:
  0.0 30.4 jit_solution(1826275587339642267)
XLA Ops:
  0.6 1.3 %pack_panels.1 = (f32[2,288,128]{2,1,0:T(8,128)S(1)}, f32[2,384,128]{2,1,0:T(8,128)S(1)}, f32[8,128]{1,0:T(8,128)S(1)}, f32[2,96,128]{2,1,0:T(8,128)S(1)}, f32[2...) custom-call(s32[4,4]{1,0:T(4,128)} %pat.1, f32[2,32,512]{2,1,0:T(8,128)} %a_hbm.1, f32[2,128,128]{2,1,0:T(8,128)} %t_hbm.1, ...), custom_call_target="tpu_custom_call" | custom-call | flops 1000000 | bytes 1000 | tf_op jit(solution)/shard_map/pack_panels/pallas_call | solution.py:68
  1.9 3.0 %collective-permute-start.6 = (f32[2,288,128]{2,1,0:T(8,128)S(1)}, f32[2,288,128]{2,1,0:T(8,128)S(1)}, u32[]{:S(2)}, u32[]{:S(2)}) collective-permute-start(f32[2,288,128]{2,1,0:T(8,128)S(1)} %get-tuple-element.60.top0), channel_id=1, source_target_pairs={{0,2},{1,3},{2,0},{3,1},{4,6},{5,7},{6,4},{7,5},{8,10},{9,11},{10,... | collective-permute-start | bytes 884744 | tf_op jit(solution)/shard_map/ppermute | solution.py:15
  4.9 1.6 %collective-permute-start = (f32[2,96,128]{2,1,0:T(8,128)S(1)}, f32[2,96,128]{2,1,0:T(8,128)S(1)}, u32[]{:S(2)}, u32[]{:S(2)}) collective-permute-start(f32[2,96,128]{2,1,0:T(8,128)S(1)} %get-tuple-element.46), channel_id=1, source_target_pairs={{0,4},{1,5},{2,6},{3,7},{4,0},{5,1},{6,2},{7,3},{8,12},{9,13},{10,... | collective-permute-start | bytes 294920 | tf_op jit(solution)/shard_map/ppermute | solution.py:15
  6.5 2.6 %collective-permute-start.1 = (f32[2,64,128]{2,1,0:T(8,128)S(1)}, f32[2,64,128]{2,1,0:T(8,128)S(1)}, u32[]{:S(2)}, u32[]{:S(2)}) collective-permute-start(f32[2,64,128]{2,1,0:T(8,128)S(1)} %get-tuple-element.47), channel_id=1, source_target_pairs={{0,8},{1,9},{2,10},{3,11},{4,12},{5,13},{6,14},{7,15},{8,0},{9,1},... | collective-permute-start | bytes 196616 | tf_op jit(solution)/shard_map/ppermute | solution.py:15
  9.1 0.2 collective-permute-start.2
  9.3 1.7 %prep.1 = (f32[2,1536,128]{2,1,0:T(8,128)S(1)}, f32[2,384,128]{2,1,0:T(8,128)S(1)}, bf16[3,512,256]{2,1,0:T(8,128)(2,1)S(1)}, bf16[3,512,256]{2,1,0:T(8,128)(2,1...) custom-call(f32[2,1536,128]{2,1,0:T(8,128)} %panel.1, f32[2,384,128]{2,1,0:T(8,128)} %link_c.1, ...), custom_call_target="tpu_custom_call" | custom-call | flops 1000000 | bytes 1000 | tf_op jit(solution)/shard_map/prep/pallas_call | solution.py:148
  11.1 3.7 %collective-permute-done.2.z3 = f32[2,32,128]{2,1,0:T(8,128)S(1)} collective-permute-done((f32[2,32,128]{2,1,0:T(8,128)S(1)}, f32[2,32,128]{2,1,0:T(8,128)S(1)}, u32[]{:S(2)}, u32[]{:S(2)}) %collective-permute-start.2) | collective-permute-done | bytes 32800 | tf_op jit(solution)/shard_map/ppermute | solution.py:15
  14.8 0.0 collective-permute-done.1.z2
  14.8 0.0 collective-permute-done.z1
  14.8 0.0 collective-permute-start.8
  14.8 0.5 %collective-permute-start.5 = (f32[2,288,128]{2,1,0:T(8,128)S(1)}, f32[2,288,128]{2,1,0:T(8,128)S(1)}, u32[]{:S(2)}, u32[]{:S(2)}) collective-permute-start(f32[2,288,128]{2,1,0:T(8,128)S(1)} %get-tuple-element.60.top0), channel_id=1, source_target_pairs={{0,1},{1,0},{2,3},{3,2},{4,5},{5,4},{6,7},{7,6},{8,9},{9,8},{10,11... | collective-permute-start | bytes 884744 | tf_op jit(solution)/shard_map/ppermute | solution.py:15
  15.3 0.0 collective-permute-done.6.top2
  15.3 0.1 collective-permute-start.7
  15.4 0.6 %collective-permute-start.4 = (f32[2,192,128]{2,1,0:T(8,128)S(1)}, f32[2,192,128]{2,1,0:T(8,128)S(1)}, u32[]{:S(2)}, u32[]{:S(2)}) collective-permute-start(f32[2,192,128]{2,1,0:T(8,128)S(1)} %join_root.1.b0), channel_id=1, source_target_pairs={{0,2},{1,3},{2,0},{3,1},{4,6},{5,7},{6,4},{7,5},{8,10},{9,11},{10,... | collective-permute-start | bytes 589832 | tf_op jit(solution)/shard_map/ppermute | solution.py:15
  16.0 0.2 collective-permute-start.3
  16.1 0.8 %collective-permute-done.5.top1 = f32[2,288,128]{2,1,0:T(8,128)S(1)} collective-permute-done((f32[2,288,128]{2,1,0:T(8,128)S(1)}, f32[2,288,128]{2,1,0:T(8,128)S(1)}, u32[]{:S(2)}, u32[]{:S(2)}) %collective-permute-start.5) | collective-permute-done | bytes 294944 | tf_op jit(solution)/shard_map/ppermute | solution.py:15
  16.9 0.0 collective-permute-done.8.mid1
  17.0 0.4 %collective-permute-done.7.top3 = f32[2,288,128]{2,1,0:T(8,128)S(1)} collective-permute-done((f32[2,288,128]{2,1,0:T(8,128)S(1)}, f32[2,288,128]{2,1,0:T(8,128)S(1)}, u32[]{:S(2)}, u32[]{:S(2)}) %collective-permute-start.7) | collective-permute-done | bytes 294944 | tf_op jit(solution)/shard_map/ppermute | solution.py:15
  17.4 5.6 %front.1 = (bf16[5,1024,256]{2,1,0:T(8,128)(2,1)S(1)}, bf16[5,1024,256]{2,1,0:T(8,128)(2,1)S(1)}, bf16[512,512]{1,0:T(8,128)(2,1)S(1)}, bf16[512,512]{1,0:T(8,12...) custom-call(f32[8,128]{1,0:T(8,128)S(1)} %get-tuple-element.45.mask_, ...), custom_call_target="tpu_custom_call" | custom-call | flops 1000000 | bytes 1000 | tf_op jit(solution)/shard_map/front/pallas_call | solution.py:273
  22.9 0.0 collective-permute-done.4.b2
  23.0 0.2 collective-permute-start.9
  23.2 0.0 collective-permute-done.3.b1
  23.2 1.3 %collective-permute-done.9.b3 = f32[2,192,128]{2,1,0:T(8,128)S(1)} collective-permute-done((f32[2,192,128]{2,1,0:T(8,128)S(1)}, f32[2,192,128]{2,1,0:T(8,128)S(1)}, u32[]{:S(2)}, u32[]{:S(2)}) %collective-permute-start.9) | collective-permute-done | bytes 196640 | tf_op jit(solution)/shard_map/ppermute | solution.py:15
  24.5 6.0 %back.1 = (f32[2,128,128]{2,1,0:T(8,128)}, f32[2,32,128]{2,1,0:T(8,128)}, f32[2,256,128]{2,1,0:T(8,128)}, f32[2,64,128]{2,1,0:T(8,128)}, f32[2,64,128]{2,1,0:T(8...) custom-call(f32[8,128]{1,0:T(8,128)S(1)} %get-tuple-element.45.mask_r, ...), custom_call_target="tpu_custom_call" | custom-call | flops 8000000000 | bytes 12000000 | tf_op jit(solution)/shard_map/back/pallas_call | solution.py:387
  (1 shorter events, 0.0 us)
Async XLA Ops:
  1.9 13.4 %collective-permute-start.6 = (f32[2,288,128]{2,1,0:T(8,128)S(1)}, f32[2,288,128]{2,1,0:T(8,128)S(1)}, u32[]{:S(2)}, u32[]{:S(2)}) collective-permute-start(f32[2,288,128]{2,1,0:T(8,128)S(1)} %get-tuple-element.60.top0), channel_id=1, source_target_pairs={{0,2},{1,3},{2,0},{3,1},{4,6},{5,7},{6,4},{7,5},{8,10},{9,11},{10,... | collective-permute-start | bytes 884744 | tf_op jit(solution)/shard_map/ppermute | solution.py:15
  4.9 9.9 %collective-permute-start = (f32[2,96,128]{2,1,0:T(8,128)S(1)}, f32[2,96,128]{2,1,0:T(8,128)S(1)}, u32[]{:S(2)}, u32[]{:S(2)}) collective-permute-start(f32[2,96,128]{2,1,0:T(8,128)S(1)} %get-tuple-element.46), channel_id=1, source_target_pairs={{0,4},{1,5},{2,6},{3,7},{4,0},{5,1},{6,2},{7,3},{8,12},{9,13},{10,... | collective-permute-start | bytes 294920 | tf_op jit(solution)/shard_map/ppermute | solution.py:15
  6.5 8.3 %collective-permute-start.1 = (f32[2,64,128]{2,1,0:T(8,128)S(1)}, f32[2,64,128]{2,1,0:T(8,128)S(1)}, u32[]{:S(2)}, u32[]{:S(2)}) collective-permute-start(f32[2,64,128]{2,1,0:T(8,128)S(1)} %get-tuple-element.47), channel_id=1, source_target_pairs={{0,8},{1,9},{2,10},{3,11},{4,12},{5,13},{6,14},{7,15},{8,0},{9,1},... | collective-permute-start | bytes 196616 | tf_op jit(solution)/shard_map/ppermute | solution.py:15
  9.1 5.7 %collective-permute-start.2 = (f32[2,32,128]{2,1,0:T(8,128)S(1)}, f32[2,32,128]{2,1,0:T(8,128)S(1)}, u32[]{:S(2)}, u32[]{:S(2)}) collective-permute-start(f32[2,32,128]{2,1,0:T(8,128)S(1)} %get-tuple-element.48), channel_id=1, source_target_pairs={{0,12},{1,13},{2,14},{3,15},{4,8},{5,9},{6,10},{7,11},{8,4},{9,5},... | collective-permute-start | bytes 98312 | tf_op jit(solution)/shard_map/ppermute | solution.py:15
  14.8 2.1 %collective-permute-start.8 = (f32[2,384,128]{2,1,0:T(8,128)S(1)}, f32[2,384,128]{2,1,0:T(8,128)S(1)}, u32[]{:S(2)}, u32[]{:S(2)}) collective-permute-start(f32[2,384,128]{2,1,0:T(8,128)S(1)} %get-tuple-element.61.mid0), channel_id=1, source_target_pairs={{0,1},{1,0},{2,3},{3,2},{4,5},{5,4},{6,7},{7,6},{8,9},{9,8},{10,11... | collective-permute-start | bytes 1179656 | tf_op jit(solution)/shard_map/ppermute | solution.py:15
  14.8 2.1 %collective-permute-start.5 = (f32[2,288,128]{2,1,0:T(8,128)S(1)}, f32[2,288,128]{2,1,0:T(8,128)S(1)}, u32[]{:S(2)}, u32[]{:S(2)}) collective-permute-start(f32[2,288,128]{2,1,0:T(8,128)S(1)} %get-tuple-element.60.top0), channel_id=1, source_target_pairs={{0,1},{1,0},{2,3},{3,2},{4,5},{5,4},{6,7},{7,6},{8,9},{9,8},{10,11... | collective-permute-start | bytes 884744 | tf_op jit(solution)/shard_map/ppermute | solution.py:15
  15.3 2.1 %collective-permute-start.7 = (f32[2,288,128]{2,1,0:T(8,128)S(1)}, f32[2,288,128]{2,1,0:T(8,128)S(1)}, u32[]{:S(2)}, u32[]{:S(2)}) collective-permute-start(f32[2,288,128]{2,1,0:T(8,128)S(1)} %collective-permute-done.6.top2), channel_id=1, source_target_pairs={{0,1},{1,0},{2,3},{3,2},{4,5},{5,4},{6,7},{7,6},{8,9},{9,8},{10,11... | collective-permute-start | bytes 884744 | tf_op jit(solution)/shard_map/ppermute | solution.py:15
  15.4 7.5 %collective-permute-start.4 = (f32[2,192,128]{2,1,0:T(8,128)S(1)}, f32[2,192,128]{2,1,0:T(8,128)S(1)}, u32[]{:S(2)}, u32[]{:S(2)}) collective-permute-start(f32[2,192,128]{2,1,0:T(8,128)S(1)} %join_root.1.b0), channel_id=1, source_target_pairs={{0,2},{1,3},{2,0},{3,1},{4,6},{5,7},{6,4},{7,5},{8,10},{9,11},{10,... | collective-permute-start | bytes 589832 | tf_op jit(solution)/shard_map/ppermute | solution.py:15
  16.0 7.2 %collective-permute-start.3 = (f32[2,192,128]{2,1,0:T(8,128)S(1)}, f32[2,192,128]{2,1,0:T(8,128)S(1)}, u32[]{:S(2)}, u32[]{:S(2)}) collective-permute-start(f32[2,192,128]{2,1,0:T(8,128)S(1)} %join_root.1.b0), channel_id=1, source_target_pairs={{0,1},{1,0},{2,3},{3,2},{4,5},{5,4},{6,7},{7,6},{8,9},{9,8},{10,11... | collective-permute-start | bytes 589832 | tf_op jit(solution)/shard_map/ppermute | solution.py:15
  23.0 1.5 %collective-permute-start.9 = (f32[2,192,128]{2,1,0:T(8,128)S(1)}, f32[2,192,128]{2,1,0:T(8,128)S(1)}, u32[]{:S(2)}, u32[]{:S(2)}) collective-permute-start(f32[2,192,128]{2,1,0:T(8,128)S(1)} %collective-permute-done.4.b2), channel_id=1, source_target_pairs={{0,1},{1,0},{2,3},{3,2},{4,5},{5,4},{6,7},{7,6},{8,9},{9,8},{10,11... | collective-permute-start | bytes 589832 | tf_op jit(solution)/shard_map/ppermute | solution.py:15

commit v2 on v1

--- a/solution.py
+++ b/solution.py
@@ -40,15 +40,16 @@
     return device // 4 if planes else device * 0
 
 
-def pack_kernel(pat, a_hbm, t_hbm, i_hbm, pm_hbm, lm_hbm, im_hbm, top, mid, masks, z1, z2, z3, pat_s, sem):
+def pack_kernel(pat, a_hbm, t_hbm, i_hbm, pm_hbm, lm_hbm, im_hbm, top, mine, masks, z1, z2, z3, pat_s, sem):
     plane = lax.axis_index("row") // 4
-    pairs = [
-        (pat, pat_s),
-        (t_hbm, top.at[:, 0:128, :]), (i_hbm, top.at[:, 128:160, :]),
-        (pm_hbm, mid.at[:, 0:256, :]), (lm_hbm, mid.at[:, 256:320, :]), (im_hbm, mid.at[:, 320:384, :]),
+    pairs = [(pat, pat_s)]
+    for dst in (top, mine):
+        pairs += [(t_hbm, dst.at[:, 0:128, :]), (i_hbm, dst.at[:, 128:160, :])]
+        for n in range(4):
+            pairs.append((a_hbm.at[:, :, n * 128 : n * 128 + 128], dst.at[:, 160 + n * 32 : 192 + n * 32, :]))
+    pairs += [
+        (pm_hbm, mine.at[:, 288:544, :]), (lm_hbm, mine.at[:, 544:608, :]), (im_hbm, mine.at[:, 608:672, :]),
     ]
-    for n in range(4):
-        pairs.append((a_hbm.at[:, :, n * 128 : n * 128 + 128], top.at[:, 160 + n * 32 : 192 + n * 32, :]))
     for dst, order in ((z1, (0, 3, 2)), (z2, (0, 1)), (z3, (0,))):
         for n, apart in enumerate(order):
             pairs.append((a_hbm.at[:, :, at((plane ^ apart) * 128, 128)], dst.at[:, n * 32 : n * 32 + 32, :]))
@@ -64,31 +65,33 @@
 
 
 def pack(pattern, *mine):
-    shapes = [(2, 288, 128), (2, 384, 128), (8, 128), (2, 96, 128), (2, 64, 128), (2, 32, 128)]
+    shapes = [(2, 288, 128), (2, 672, 128), (8, 128), (2, 96, 128), (2, 64, 128), (2, 32, 128)]
     return pl.pallas_call(
         pack_kernel,
         out_shape=tuple(jax.ShapeDtypeStruct(s, F32) for s in shapes),
         in_specs=[ANY] * 7,
         out_specs=(VMEM,) * len(shapes),
-        scratch_shapes=[pltpu.SMEM(pattern.shape, jnp.int32), pltpu.SemaphoreType.DMA((16,))],
+        scratch_shapes=[pltpu.SMEM(pattern.shape, jnp.int32), pltpu.SemaphoreType.DMA((22,))],
         compiler_params=pltpu.CompilerParams(vmem_limit_bytes=4 << 20),
         cost_estimate=pl.CostEstimate(flops=1_000_000, bytes_accessed=1_000, transcendentals=0),
         name="pack_panels",
     )(in_hbm(pattern), *(in_hbm(x) for x in mine))
 
 
-def join_kernel(z1, z2, z3, joined):
-    joined[:, 0:96, :] = z1[...]
-    joined[:, 96:160, :] = z2[...]
-    joined[:, 160:192, :] = z3[...]
+def join_kernel(z1, z2, z3, far_top, near, both):
+    for ref in (near, both):
+        ref[:, 0:96, :] = z1[...]
+        ref[:, 96:160, :] = z2[...]
+        ref[:, 160:192, :] = z3[...]
+    both[:, 192:480, :] = far_top[...]
 
 
 def join(*blocks):
     return pl.pallas_call(
         join_kernel,
-        out_shape=jax.ShapeDtypeStruct((2, 192, 128), F32),
-        in_specs=[VMEM] * 3,
-        out_specs=VMEM,
+        out_shape=(jax.ShapeDtypeStruct((2, 192, 128), F32), jax.ShapeDtypeStruct((2, 480, 128), F32)),
+        in_specs=[VMEM] * 4,
+        out_specs=(VMEM, VMEM),
         compiler_params=pltpu.CompilerParams(vmem_limit_bytes=4 << 20),
         cost_estimate=pl.CostEstimate(flops=1_000_000, bytes_accessed=1_000, transcendentals=0),
         name="join_root",
@@ -157,11 +160,16 @@
     )(in_hbm(panel), in_hbm(link_c), in_hbm(link_e), in_hbm(inv))
 
 
+def own_columns(j, row_h, row_l, col_h, col_l, x_h, x_l, out, first=0):
+    out[j - first, 0:128] = mm3(row_h[...], row_l[...], x_h[j], x_l[j])
+    out[j - first, 128:512] = mm3(col_h[...], col_l[...], x_h[j, 0:256], x_l[j, 0:256])
+
+
 def make_front_kernel(planes, leaves):
     def kernel(
-        mask_ref, top0, top1, top2, top3, mid0, mid1, g_s, li_s, rhs_h, rhs_l, auxl_h, auxl_l,
-        x_h, x_l, tt_h, tt_l, tl_h, tl_l, base_top, base_leaf, c_own,
-        l_s, b_s, t0_s, am_s, d_s, own, row_h, row_l, col_h, col_l,
+        mask_ref, mine, other, both, both_other, g_s, li_s, rhs_h, rhs_l, auxl_h, auxl_l,
+        x_h, x_l, tt_h, tt_l, tl_h, tl_l, base_top, base_leaf, row_h, row_l, col_h, col_l, c_top,
+        l_s, b_s, t0_s, am_s, d_s, own,
         lhs_h, lhs_l, ra_h, ra_l, rq_h, rq_l, aux_h, aux_l, rrs_h, rrs_l,
     ):
         device = lax.axis_index("row")
@@ -171,33 +179,24 @@
         def rel(supernode):
             return at((supernode ^ plane) * 128, 128)
 
-        for k, ref in enumerate((top0, top1, top2, top3)):
+        for k, (ref, row) in enumerate(((mine, 0), (other, 0), (both, 192), (both_other, 192))):
             q = quarter ^ k
-            l_s[:, rel(q), :] = ref[:, 0:128, :]
-            t0_s[:, at(q * 32, 32), :] = ref[:, 128:160, :]
+            l_s[:, rel(q), :] = ref[:, row : row + 128, :]
+            t0_s[:, at(q * 32, 32), :] = ref[:, row + 128 : row + 160, :]
             for n in range(4):
-                own[:, at(q * 32, 32), n * 128 : n * 128 + 128] = ref[:, 160 + n * 32 : 192 + n * 32, :]
-        for k, ref in enumerate((mid0, mid1)):
+                own[:, at(q * 32, 32), n * 128 : n * 128 + 128] = (
+                    ref[:, row + 160 + n * 32 : row + 192 + n * 32, :]
+                )
+        for k, ref in enumerate((mine, other)):
             h = half ^ k
             for n in (0, 1):
-                b_s[:, rel(h * 2 + n), :] = ref[:, n * 128 : n * 128 + 128, :]
-            am_s[:, at(h * 64, 64), :] = ref[:, 256:320, :]
-            d_s[:, at(h * 64, 64), :] = ref[:, 320:384, :]
+                b_s[:, rel(h * 2 + n), :] = ref[:, 288 + n * 128 : 416 + n * 128, :]
+            am_s[:, at(h * 64, 64), :] = ref[:, 544:608, :]
+            d_s[:, at(h * 64, 64), :] = ref[:, 608:672, :]
         masks = [mask_ref[r : r + 1, :] for r in range(4)]
 
         def put_x(j, r, re, im):
             put_rhs(x_h.at[j], x_l.at[j], r * 256, re, im)
-
-        for r in range(4):
-            cols = at((plane ^ r) * 128, 128)
-            re, im = own[0, :, cols], own[1, :, cols]
-            put_pair(row_h, row_l, 0, r * 256, re, im)
-            if r:
-                put_pair(col_h, col_l, (r - 1) * 128, 0, re.T, im.T)
-
-        def own_product(j):
-            c_own[j, 0:128] = mm3(row_h[...], row_l[...], x_h[j], x_l[j])
-            c_own[j, 128:512] = mm3(col_h[...], col_l[...], x_h[j, 0:256], x_l[j, 0:256])
 
         put_rhs(ra_h, ra_l, 0, am_s[0], am_s[1])
         for r in range(4):
@@ -231,8 +230,14 @@
         base_top[2, 0] = d_r
         base_top[2, 1] = d_i
 
-        own_product(0)
-        own_product(1)
+        for r in range(4):
+            cols = at((plane ^ r) * 128, 128)
+            re, im = own[0, :, cols], own[1, :, cols]
+            put_pair(row_h, row_l, 0, r * 256, re, im)
+            if r:
+                put_pair(col_h, col_l, (r - 1) * 128, 0, re.T, im.T)
+        for j in (0, 1):
+            own_columns(j, row_h, row_l, col_h, col_l, x_h, x_l, c_top)
         for j in range(leaves):
             got = mm3(lhs_h[...], lhs_l[...], rhs_h[j], rhs_l[j])
             for r in range(4):
@@ -255,43 +260,60 @@
             got = mm3(auxl_h[j], auxl_l[j], rrs_h[j], rrs_l[j])
             base_leaf[j, 2, 0] = li_s[0, mine] - got[:, 0:128]
             base_leaf[j, 2, 1] = li_s[1, mine] - got[:, 128:256]
-            own_product(2 + j)
 
     return kernel
 
 
-def front(planes, masks, tops, mids, prepared):
+def front(planes, masks, pieces, prepared):
     leaves = prepared[0].shape[1] // 512
     n = leaves + 2
     v = pltpu.VMEM
     out = [
         ((n, 1024, 256), BF16), ((n, 1024, 256), BF16), ((512, 512), BF16), ((512, 512), BF16),
         ((leaves, 256, 512), BF16), ((leaves, 256, 512), BF16),
-        ((3, 2, 128, 128), F32), ((leaves, 3, 2, 128, 128), F32), ((n, 512, 256), F32),
+        ((3, 2, 128, 128), F32), ((leaves, 3, 2, 128, 128), F32),
+        ((128, 1024), BF16), ((128, 1024), BF16), ((384, 256), BF16), ((384, 256), BF16),
+        ((2, 512, 256), F32),
     ]
     pair = lambda *shape: [v(shape, BF16)] * 2
     return pl.pallas_call(
         make_front_kernel(planes, leaves),
         out_shape=tuple(jax.ShapeDtypeStruct(s, d) for s, d in out),
-        in_specs=[VMEM] * 13,
+        in_specs=[VMEM] * 11,
         out_specs=(VMEM,) * len(out),
         scratch_shapes=[
             v((2, 512, 128), F32), v((2, 512, 128), F32),
             v((2, 128, 128), F32), v((2, 128, 128), F32), v((2, 128, 128), F32),
-            v((2, 128, 512), F32), *pair(128, 1024), *pair(384, 256),
-            *pair(768, 512), *pair(256, 256), *pair(256, 256), *pair(128, 256),
+            v((2, 128, 512), F32), *pair(768, 512), *pair(256, 256), *pair(256, 256), *pair(128, 256),
             *pair(leaves, 512, 256),
         ],
         compiler_params=pltpu.CompilerParams(vmem_limit_bytes=24 << 20),
         cost_estimate=pl.CostEstimate(flops=1_000_000, bytes_accessed=1_000, transcendentals=0),
         name="front",
-    )(masks, *tops, *mids, *prepared)
+    )(masks, *pieces, *prepared)
+
+
+def own_kernel(row_h, row_l, col_h, col_l, x_h, x_l, c_leaf):
+    for j in range(2, x_h.shape[0]):
+        own_columns(j, row_h, row_l, col_h, col_l, x_h, x_l, c_leaf, 2)
+
+
+def own_product(row_h, row_l, col_h, col_l, x_h, x_l):
+    return pl.pallas_call(
+        own_kernel,
+        out_shape=jax.ShapeDtypeStruct((x_h.shape[0] - 2, 512, 256), F32),
+        in_specs=[VMEM] * 6,
+        out_specs=VMEM,
+        compiler_params=pltpu.CompilerParams(vmem_limit_bytes=12 << 20),
+        cost_estimate=pl.CostEstimate(flops=1_000_000, bytes_accessed=1_000, transcendentals=0),
+        name="own_product",
+    )(row_h, row_l, col_h, col_l, x_h, x_l)
 
 
 def make_back_kernel(planes, leaves):
     def kernel(
         mask_ref, b0, b1, b2, b3,
-        x_h, x_l, tt_h, tt_l, tl_h, tl_l, base_top, base_leaf, c_own,
+        x_h, x_l, tt_h, tt_l, tl_h, tl_l, base_top, base_leaf, c_top, c_leaf,
         col_top, diag_top, col_mid, cross_mid, diag_mid, col_leaf, cross_c, cross_e, diag_leaf,
         blocks, a_h, a_l, cb_h, cb_l, c_s, d_s, e_s, f_s, top_s, mid_s, sem,
     ):
@@ -324,7 +346,7 @@
                 place = at((plane ^ r) * 128, 128)
                 for part in (0, 1):
                     lanes = slice(part * 128, part * 128 + 128)
-                    c = c_own[j, rows, lanes]
+                    c = c_leaf[j - 2, rows, lanes] if j > 1 else c_top[j, rows, lanes]
                     if r:
                         c = c + got[r * 128 - 128 : r * 128, lanes]
                     c = c * masks[r]
@@ -424,32 +446,28 @@
     leaves = panel_leaf.shape[1] // 512
     prepared = prep(panel_leaf, link_leaf_mid, link_leaf_top, inv_leaf)
     if planes:
-        top, mid, masks, *sent = pack(
+        top, mine, masks, *sent = pack(
             pattern, ainv_root, panel_top, inv_top, panel_mid, link_mid, inv_mid
         )
         got = [swap(x, 4 * k) for k, x in zip((1, 2, 3), sent)]
-        *got, top_1, mid_1 = lax.optimization_barrier((*got, top, mid, *prepared))[:5]
-        far_top = swap(top, 2)
-        tops = [top, swap(top_1, 1), far_top, swap(far_top, 1)]
-        mids = [mid, swap(mid_1, 1)]
-        near = join(*got)
+        *got, _ = lax.optimization_barrier((*got, *prepared))[:4]
+        near, both = join(*got, swap(top, 2))
         far = swap(near, 2)
-        root = [near, swap(near, 1)]
     else:
-        mid = jnp.concatenate([panel_mid, link_mid, inv_mid], axis=1)
         node = lax.dynamic_index_in_dim(pattern, lax.axis_index("row") // 4, 0, keepdims=False)
         masks = jnp.broadcast_to(jnp.pad(node.astype(F32), (0, 4))[:, None], (8, 128))
         own, root = root_gathered(ainv_root)
         own = [own[:, :, n * 128 : n * 128 + 128] for n in range(4)]
         top = jnp.concatenate([panel_top, inv_top, *own], axis=1)
-        far_top = swap(top, 2)
-        tops = [top, swap(top, 1), far_top, swap(far_top, 1)]
-        mids = [mid, swap(mid, 1)]
-    firsts = front(planes, masks, tops, mids, prepared)
+        mine = jnp.concatenate([top, panel_mid, link_mid, inv_mid], axis=1)
+        both = jnp.concatenate([root[0], swap(top, 2)], axis=1)
+    pieces = [mine, swap(mine, 1), both, swap(both, 1)]
+    firsts = front(planes, masks, pieces, prepared)
     if planes:
         far, *firsts = lax.optimization_barrier((far, *firsts))
-        root += [far, swap(far, 1)]
-    return back(planes, masks, root, firsts, leaves)
+        root = [both, pieces[3], far, swap(far, 1)]
+    c_leaf = own_product(*firsts[8:12], *firsts[:2])
+    return back(planes, masks, root, [*firsts[:8], firsts[12], c_leaf], leaves)
 
 
 def solution(mesh):

time: 30.6 us -> 30.1 us (0.984)
  starting transfers between devices: 8.93 us -> 8.07 us
  Pallas kernels: 14.5 us -> 15 us
    pallas_call x1 -> x2, Pallas kernels: 0.01 us -> 1.29 us  [the longest x1 1.24 us: own_product(): pl.pallas_call(own_kernel, out_shape=jax.ShapeDtypeStruct((x_h.shape[0] -...]
    pallas_call x1, Pallas kernels: 5.57 us -> 4.52 us  [front(): pl.pallas_call(make_front_kernel(planes, leaves), out_shape=tuple((jax.Sh...]
    ppermute x10 -> x8, starting transfers between devices: 8.93 us -> 8.07 us  [swap(): lax.ppermute(x, 'row', [(i, i ^ apart) for i in range(lax.axis_size('row'...]
    ppermute x10 -> x8, waiting for transfers between devices: 6.27 us -> 6.16 us  [swap(): lax.ppermute(x, 'row', [(i, i ^ apart) for i in range(lax.axis_size('row'...]
  transfers between devices with their start and end apart: 10 -> 8, of which waited for: 4 -> 4; matrix products, arithmetic and copies ran while one was open for 0% -> 0% of each run, Pallas kernels for 24% -> 25%
where the time goes in v2:
time: 30.1 us; the launch traced here: 29.9 us
  Pallas kernels  15 us (50%)
  starting transfers between devices  8.07 us (27%)
  waiting for transfers between devices  6.16 us (20%)
  between operations  0.7 us (2%)
    ppermute x8, starting transfers between devices, swap(): lax.ppermute(x, 'row', [(i, i ^ apart) for i in range(lax.axis_size('row'...  8.07 us
    ppermute x8, waiting for transfers between devices, swap(): lax.ppermute(x, 'row', [(i, i ^ apart) for i in range(lax.axis_size('row'...  6.16 us
    pallas_call x1, Pallas kernels, back(): pl.pallas_call(make_back_kernel(planes, leaves), out_shape=tuple((jax.Sha...  5.95 us
    pallas_call x1, Pallas kernels, front(): pl.pallas_call(make_front_kernel(planes, leaves), out_shape=tuple((jax.Sh...  4.52 us
    pallas_call x1, Pallas kernels, prep(): pl.pallas_call(make_prep_kernel(leaves), out_shape=tuple((jax.ShapeDtypeS...  1.74 us
    pallas_call x1, Pallas kernels, pack(): pl.pallas_call(pack_kernel, out_shape=tuple((jax.ShapeDtypeStruct(s, F32)...  1.47 us
    pallas_call x1, Pallas kernels, own_product(): pl.pallas_call(own_kernel, out_shape=jax.ShapeDtypeStruct((x_h.shape[0] -...  1.24 us
  transfers between devices with their start and end apart: 8, of which 4 were waited for; matrix products, arithmetic and copies ran while one was open for 0% of the time, Pallas kernels for 25%

profile of v2, /device:TPU:0, one launch (start us, length us, event | category | flops | bytes accessed | tf_op | source)
XLA Modules:
  0.0 29.9 jit_solution(5453033674142517845)
XLA Ops:
  0.6 1.5 %pack_panels.1 = (f32[2,288,128]{2,1,0:T(8,128)S(1)}, f32[2,672,128]{2,1,0:T(8,128)S(1)}, f32[8,128]{1,0:T(8,128)S(1)}, f32[2,96,128]{2,1,0:T(8,128)S(1)}, f32[2...) custom-call(s32[4,4]{1,0:T(4,128)} %pat.1, f32[2,32,512]{2,1,0:T(8,128)} %a_hbm.1, f32[2,128,128]{2,1,0:T(8,128)} %t_hbm.1, ...), custom_call_target="tpu_custom_call" | custom-call | flops 1000000 | bytes 1000 | tf_op jit(solution)/shard_map/pack_panels/pallas_call | solution.py:69
  2.1 3.0 %collective-permute-start.3 = (f32[2,288,128]{2,1,0:T(8,128)S(1)}, f32[2,288,128]{2,1,0:T(8,128)S(1)}, u32[]{:S(2)}, u32[]{:S(2)}) collective-permute-start(f32[2,288,128]{2,1,0:T(8,128)S(1)} %get-tuple-element.66), channel_id=1, source_target_pairs={{0,2},{1,3},{2,0},{3,1},{4,6},{5,7},{6,4},{7,5},{8,10},{9,11},{10,... | collective-permute-start | bytes 884744 | tf_op jit(solution)/shard_map/ppermute | solution.py:15
  5.2 0.0 collective-permute-start.6
  5.2 1.6 %collective-permute-start = (f32[2,96,128]{2,1,0:T(8,128)S(1)}, f32[2,96,128]{2,1,0:T(8,128)S(1)}, u32[]{:S(2)}, u32[]{:S(2)}) collective-permute-start(f32[2,96,128]{2,1,0:T(8,128)S(1)} %get-tuple-element.54), channel_id=1, source_target_pairs={{0,4},{1,5},{2,6},{3,7},{4,0},{5,1},{6,2},{7,3},{8,12},{9,13},{10,... | collective-permute-start | bytes 294920 | tf_op jit(solution)/shard_map/ppermute | solution.py:15
  6.7 2.6 %collective-permute-start.1 = (f32[2,64,128]{2,1,0:T(8,128)S(1)}, f32[2,64,128]{2,1,0:T(8,128)S(1)}, u32[]{:S(2)}, u32[]{:S(2)}) collective-permute-start(f32[2,64,128]{2,1,0:T(8,128)S(1)} %get-tuple-element.55), channel_id=1, source_target_pairs={{0,8},{1,9},{2,10},{3,11},{4,12},{5,13},{6,14},{7,15},{8,0},{9,1},... | collective-permute-start | bytes 196616 | tf_op jit(solution)/shard_map/ppermute | solution.py:15
  9.3 0.2 collective-permute-start.2
  9.5 1.7 %prep.1 = (f32[2,1536,128]{2,1,0:T(8,128)S(1)}, f32[2,384,128]{2,1,0:T(8,128)S(1)}, bf16[3,512,256]{2,1,0:T(8,128)(2,1)S(1)}, bf16[3,512,256]{2,1,0:T(8,128)(2,1...) custom-call(f32[2,1536,128]{2,1,0:T(8,128)} %panel.1, f32[2,384,128]{2,1,0:T(8,128)} %link_c.1, ...), custom_call_target="tpu_custom_call" | custom-call | flops 1000000 | bytes 1000 | tf_op jit(solution)/shard_map/prep/pallas_call | solution.py:151
  11.3 3.7 %collective-permute-done.2.z3 = f32[2,32,128]{2,1,0:T(8,128)S(1)} collective-permute-done((f32[2,32,128]{2,1,0:T(8,128)S(1)}, f32[2,32,128]{2,1,0:T(8,128)S(1)}, u32[]{:S(2)}, u32[]{:S(2)}) %collective-permute-start.2) | collective-permute-done | bytes 32800 | tf_op jit(solution)/shard_map/ppermute | solution.py:15
  15.0 0.0 collective-permute-done.1.z2
  15.0 0.0 collective-permute-done.z1
  15.0 0.0 collective-permute-done.3.far_top
  15.1 0.1 collective-permute-start.4
  15.2 0.6 %collective-permute-start.5 = (f32[2,192,128]{2,1,0:T(8,128)S(1)}, f32[2,192,128]{2,1,0:T(8,128)S(1)}, u32[]{:S(2)}, u32[]{:S(2)}) collective-permute-start(f32[2,192,128]{2,1,0:T(8,128)S(1)} %get-tuple-element.68), channel_id=1, source_target_pairs={{0,2},{1,3},{2,0},{3,1},{4,6},{5,7},{6,4},{7,5},{8,10},{9,11},{10,... | collective-permute-start | bytes 589832 | tf_op jit(solution)/shard_map/ppermute | solution.py:15
  15.8 0.0 collective-permute-done.6.other
  15.8 1.3 %collective-permute-done.4.both_other.b1 = f32[2,480,128]{2,1,0:T(8,128)S(1)} collective-permute-done((f32[2,480,128]{2,1,0:T(8,128)S(1)}, f32[2,480,128]{2,1,0:T(8,128)S(1)}, u32[]{:S(2)}, u32[]{:S(2)}) %collective-permute-start.4) | collective-permute-done | bytes 491552 | tf_op jit(solution)/shard_map/ppermute | solution.py:15
  17.0 4.5 %front.1 = (bf16[5,1024,256]{2,1,0:T(8,128)(2,1)S(1)}, bf16[5,1024,256]{2,1,0:T(8,128)(2,1)S(1)}, bf16[512,512]{1,0:T(8,128)(2,1)S(1)}, bf16[512,512]{1,0:T(8,12...) custom-call(f32[8,128]{1,0:T(8,128)S(1)} %get-tuple-element.53.mask_, ...), custom_call_target="tpu_custom_call" | custom-call | flops 1000000 | bytes 1000 | tf_op jit(solution)/shard_map/front/pallas_call | solution.py:279
  21.6 0.9 %collective-permute-done.5.b2 = f32[2,192,128]{2,1,0:T(8,128)S(1)} collective-permute-done((f32[2,192,128]{2,1,0:T(8,128)S(1)}, f32[2,192,128]{2,1,0:T(8,128)S(1)}, u32[]{:S(2)}, u32[]{:S(2)}) %collective-permute-start.5) | collective-permute-done | bytes 196640 | tf_op jit(solution)/shard_map/ppermute | solution.py:15
  22.5 0.0 collective-permute-start.7
  22.5 1.2 %own_product.1.c_leaf = f32[3,512,256]{2,1,0:T(8,128)S(1)} custom-call(bf16[128,1024]{1,0:T(8,128)(2,1)S(1)} %get-tuple-element.93.row_h, bf16[128,1024]{1,0:T(8,128)(2,1)S(1)} %get-tuple-element.94.row_l, bf16[384,256]{1,0:T(8,128)(2,1)S(1)} %get-tuple-element.95.col_h, bf16[384,256]{1,0:T(8,128)(2,1)S(1)} %get-tuple-element.96.col_l, ...), custom_call_target="tpu_custom_call" | custom-call | flops 1000000 | bytes 1000 | tf_op jit(solution)/shard_map/own_product/pallas_call | solution.py:302
  23.8 0.2 collective-permute-done.7.b3
  23.9 5.9 %back.1 = (f32[2,128,128]{2,1,0:T(8,128)}, f32[2,32,128]{2,1,0:T(8,128)}, f32[2,256,128]{2,1,0:T(8,128)}, f32[2,64,128]{2,1,0:T(8,128)}, f32[2,64,128]{2,1,0:T(8...) custom-call(f32[8,128]{1,0:T(8,128)S(1)} %get-tuple-element.53.mask_r, ...), custom_call_target="tpu_custom_call" | custom-call | flops 8000000000 | bytes 12000000 | tf_op jit(solution)/shard_map/back/pallas_call | solution.py:409
  (1 shorter events, 0.0 us)
Async XLA Ops:
  2.1 12.9 %collective-permute-start.3 = (f32[2,288,128]{2,1,0:T(8,128)S(1)}, f32[2,288,128]{2,1,0:T(8,128)S(1)}, u32[]{:S(2)}, u32[]{:S(2)}) collective-permute-start(f32[2,288,128]{2,1,0:T(8,128)S(1)} %get-tuple-element.66), channel_id=1, source_target_pairs={{0,2},{1,3},{2,0},{3,1},{4,6},{5,7},{6,4},{7,5},{8,10},{9,11},{10,... | collective-permute-start | bytes 884744 | tf_op jit(solution)/shard_map/ppermute | solution.py:15
  5.2 10.6 %collective-permute-start.6 = (f32[2,672,128]{2,1,0:T(8,128)S(1)}, f32[2,672,128]{2,1,0:T(8,128)S(1)}, u32[]{:S(2)}, u32[]{:S(2)}) collective-permute-start(f32[2,672,128]{2,1,0:T(8,128)S(1)} %get-tuple-element.69.mine), channel_id=1, source_target_pairs={{0,1},{1,0},{2,3},{3,2},{4,5},{5,4},{6,7},{7,6},{8,9},{9,8},{10,11... | collective-permute-start | bytes 2064392 | tf_op jit(solution)/shard_map/ppermute | solution.py:15
  5.2 9.9 %collective-permute-start = (f32[2,96,128]{2,1,0:T(8,128)S(1)}, f32[2,96,128]{2,1,0:T(8,128)S(1)}, u32[]{:S(2)}, u32[]{:S(2)}) collective-permute-start(f32[2,96,128]{2,1,0:T(8,128)S(1)} %get-tuple-element.54), channel_id=1, source_target_pairs={{0,4},{1,5},{2,6},{3,7},{4,0},{5,1},{6,2},{7,3},{8,12},{9,13},{10,... | collective-permute-start | bytes 294920 | tf_op jit(solution)/shard_map/ppermute | solution.py:15
  6.7 8.3 %collective-permute-start.1 = (f32[2,64,128]{2,1,0:T(8,128)S(1)}, f32[2,64,128]{2,1,0:T(8,128)S(1)}, u32[]{:S(2)}, u32[]{:S(2)}) collective-permute-start(f32[2,64,128]{2,1,0:T(8,128)S(1)} %get-tuple-element.55), channel_id=1, source_target_pairs={{0,8},{1,9},{2,10},{3,11},{4,12},{5,13},{6,14},{7,15},{8,0},{9,1},... | collective-permute-start | bytes 196616 | tf_op jit(solution)/shard_map/ppermute | solution.py:15
  9.3 5.7 %collective-permute-start.2 = (f32[2,32,128]{2,1,0:T(8,128)S(1)}, f32[2,32,128]{2,1,0:T(8,128)S(1)}, u32[]{:S(2)}, u32[]{:S(2)}) collective-permute-start(f32[2,32,128]{2,1,0:T(8,128)S(1)} %get-tuple-element.56), channel_id=1, source_target_pairs={{0,12},{1,13},{2,14},{3,15},{4,8},{5,9},{6,10},{7,11},{8,4},{9,5},... | collective-permute-start | bytes 98312 | tf_op jit(solution)/shard_map/ppermute | solution.py:15
  15.1 1.9 %collective-permute-start.4 = (f32[2,480,128]{2,1,0:T(8,128)S(1)}, f32[2,480,128]{2,1,0:T(8,128)S(1)}, u32[]{:S(2)}, u32[]{:S(2)}) collective-permute-start(f32[2,480,128]{2,1,0:T(8,128)S(1)} %get-tuple-element.67.both.b0), channel_id=1, source_target_pairs={{0,1},{1,0},{2,3},{3,2},{4,5},{5,4},{6,7},{7,6},{8,9},{9,8},{10,11... | collective-permute-start | bytes 1474568 | tf_op jit(solution)/shard_map/ppermute | solution.py:15
  15.2 7.3 %collective-permute-start.5 = (f32[2,192,128]{2,1,0:T(8,128)S(1)}, f32[2,192,128]{2,1,0:T(8,128)S(1)}, u32[]{:S(2)}, u32[]{:S(2)}) collective-permute-start(f32[2,192,128]{2,1,0:T(8,128)S(1)} %get-tuple-element.68), channel_id=1, source_target_pairs={{0,2},{1,3},{2,0},{3,1},{4,6},{5,7},{6,4},{7,5},{8,10},{9,11},{10,... | collective-permute-start | bytes 589832 | tf_op jit(solution)/shard_map/ppermute | solution.py:15
  22.5 1.4 %collective-permute-start.7 = (f32[2,192,128]{2,1,0:T(8,128)S(1)}, f32[2,192,128]{2,1,0:T(8,128)S(1)}, u32[]{:S(2)}, u32[]{:S(2)}) collective-permute-start(f32[2,192,128]{2,1,0:T(8,128)S(1)} %collective-permute-done.5.b2), channel_id=1, source_target_pairs={{0,1},{1,0},{2,3},{3,2},{4,5},{5,4},{6,7},{7,6},{8,9},{9,8},{10,11... | collective-permute-start | bytes 589832 | tf_op jit(solution)/shard_map/ppermute | solution.py:15

commit v3 on v2

--- a/solution.py
+++ b/solution.py
@@ -40,62 +40,90 @@
     return device // 4 if planes else device * 0
 
 
-def pack_kernel(pat, a_hbm, t_hbm, i_hbm, pm_hbm, lm_hbm, im_hbm, top, mine, masks, z1, z2, z3, pat_s, sem):
+def pack_kernel(
+    pat, a_hbm, t_hbm, i_hbm, pm_hbm, lm_hbm, im_hbm, top, mine, masks, z1, z2, z3, a, pat_s, sem
+):
     plane = lax.axis_index("row") // 4
-    pairs = [(pat, pat_s)]
-    for dst in (top, mine):
-        pairs += [(t_hbm, dst.at[:, 0:128, :]), (i_hbm, dst.at[:, 128:160, :])]
-        for n in range(4):
-            pairs.append((a_hbm.at[:, :, n * 128 : n * 128 + 128], dst.at[:, 160 + n * 32 : 192 + n * 32, :]))
-    pairs += [
+    pairs = (
+        (a_hbm, a), (t_hbm, mine.at[:, 0:128, :]), (i_hbm, mine.at[:, 128:160, :]), (pat, pat_s),
         (pm_hbm, mine.at[:, 288:544, :]), (lm_hbm, mine.at[:, 544:608, :]), (im_hbm, mine.at[:, 608:672, :]),
-    ]
-    for dst, order in ((z1, (0, 3, 2)), (z2, (0, 1)), (z3, (0,))):
-        for n, apart in enumerate(order):
-            pairs.append((a_hbm.at[:, :, at((plane ^ apart) * 128, 128)], dst.at[:, n * 32 : n * 32 + 32, :]))
+    )
     copies = [pltpu.make_async_copy(src, dst, sem.at[n]) for n, (src, dst) in enumerate(pairs)]
     for copy in copies:
         copy.start()
     copies[0].wait()
+    for dst in (top, mine):
+        for n in range(4):
+            dst[:, 160 + n * 32 : 192 + n * 32, :] = a[:, :, n * 128 : n * 128 + 128]
+    for dst, order in ((z1, (0, 3, 2)), (z2, (0,)), (z3, (0, 1))):
+        for n, apart in enumerate(order):
+            dst[:, n * 32 : n * 32 + 32, :] = a[:, :, at((plane ^ apart) * 128, 128)]
+    copies[1].wait()
+    copies[2].wait()
+    top[:, 0:160, :] = mine[:, 0:160, :]
+    copies[3].wait()
     for r in range(4):
         masks[r : r + 1, :] = jnp.full((1, 128), pat_s[plane, plane ^ r], jnp.int32).astype(F32)
     masks[4:8, :] = jnp.zeros((4, 128), F32)
-    for copy in copies[1:]:
+    for copy in copies[4:]:
         copy.wait()
 
 
 def pack(pattern, *mine):
-    shapes = [(2, 288, 128), (2, 672, 128), (8, 128), (2, 96, 128), (2, 64, 128), (2, 32, 128)]
+    shapes = [(2, 288, 128), (2, 672, 128), (8, 128), (2, 96, 128), (2, 32, 128), (2, 64, 128)]
     return pl.pallas_call(
         pack_kernel,
         out_shape=tuple(jax.ShapeDtypeStruct(s, F32) for s in shapes),
         in_specs=[ANY] * 7,
         out_specs=(VMEM,) * len(shapes),
-        scratch_shapes=[pltpu.SMEM(pattern.shape, jnp.int32), pltpu.SemaphoreType.DMA((22,))],
+        scratch_shapes=[
+            pltpu.VMEM(mine[0].shape, F32), pltpu.SMEM(pattern.shape, jnp.int32), pltpu.SemaphoreType.DMA((7,)),
+        ],
         compiler_params=pltpu.CompilerParams(vmem_limit_bytes=4 << 20),
         cost_estimate=pl.CostEstimate(flops=1_000_000, bytes_accessed=1_000, transcendentals=0),
         name="pack_panels",
     )(in_hbm(pattern), *(in_hbm(x) for x in mine))
 
 
-def join_kernel(z1, z2, z3, far_top, near, both):
-    for ref in (near, both):
-        ref[:, 0:96, :] = z1[...]
-        ref[:, 96:160, :] = z2[...]
-        ref[:, 160:192, :] = z3[...]
+def join_kernel(z1, z2, z3, far_top, lead, rest, both):
+    plane = lax.axis_index("row") // 4
+    for n, apart in enumerate((0, 3, 2)):
+        lead[:, n * 32 : n * 32 + 32, :] = far_top[:, at(160 + (plane ^ apart) * 32, 32), :]
+    rest[:, 0:32, :] = z2[...]
+    rest[:, 32:96, :] = z3[...]
+    both[:, 0:96, :] = z1[...]
+    both[:, 96:128, :] = z2[...]
+    both[:, 128:192, :] = z3[...]
     both[:, 192:480, :] = far_top[...]
 
 
 def join(*blocks):
     return pl.pallas_call(
         join_kernel,
-        out_shape=(jax.ShapeDtypeStruct((2, 192, 128), F32), jax.ShapeDtypeStruct((2, 480, 128), F32)),
+        out_shape=tuple(jax.ShapeDtypeStruct((2, rows, 128), F32) for rows in (96, 96, 480)),
         in_specs=[VMEM] * 4,
-        out_specs=(VMEM, VMEM),
+        out_specs=(VMEM,) * 3,
         compiler_params=pltpu.CompilerParams(vmem_limit_bytes=4 << 20),
         cost_estimate=pl.CostEstimate(flops=1_000_000, bytes_accessed=1_000, transcendentals=0),
         name="join_root",
     )(*blocks)
+
+
+def stack_kernel(upper, lower, joined):
+    joined[:, 0:96, :] = upper[...]
+    joined[:, 96:192, :] = lower[...]
+
+
+def stack(upper, lower):
+    return pl.pallas_call(
+        stack_kernel,
+        out_shape=jax.ShapeDtypeStruct((2, 192, 128), F32),
+        in_specs=[VMEM] * 2,
+        out_specs=VMEM,
+        compiler_params=pltpu.CompilerParams(vmem_limit_bytes=4 << 20),
+        cost_estimate=pl.CostEstimate(flops=1_000_000, bytes_accessed=1_000, transcendentals=0),
+        name="stack_root",
+    )(upper, lower)
 
 
 def put_rhs(ref_h, ref_l, row, re, im):
@@ -160,95 +188,176 @@
     )(in_hbm(panel), in_hbm(link_c), in_hbm(link_e), in_hbm(inv))
 
 
-def own_columns(j, row_h, row_l, col_h, col_l, x_h, x_l, out, first=0):
-    out[j - first, 0:128] = mm3(row_h[...], row_l[...], x_h[j], x_l[j])
-    out[j - first, 128:512] = mm3(col_h[...], col_l[...], x_h[j, 0:256], x_l[j, 0:256])
+def put_block(x_h, x_l, t_h, t_l, row, e, re, im):
+    put_rhs(x_h, x_l, e * 256, re, im)
+    put_transposed(t_h, t_l, row, e, re, im)
+
+
+def places(planes):
+    device = lax.axis_index("row")
+    plane = own_plane(device, planes)
+    shift = plane ^ (device % 4)
+    return plane, shift // 2, shift % 2 == 1
+
+
+def mid_blocks(planes, mine, other, b_s, am_s, ra_h, ra_l):
+    plane = places(planes)[0]
+    half = lax.axis_index("row") % 2
+    for k, ref in enumerate((mine, other)):
+        h = half ^ k
+        for n in (0, 1):
+            place = at(((h * 2 + n) ^ plane) * 128, 128)
+            b_s[:, place, :] = ref[:, 288 + n * 128 : 416 + n * 128, :]
+        am_s[:, at(h * 64, 64), :] = ref[:, 544:608, :]
+    put_rhs(ra_h, ra_l, 0, am_s[0], am_s[1])
+
+
+def top_block(e, swapped, first, second, row, mask):
+    left, right = (second, first) if e == 0 else (first, second)
+    return tuple(
+        jnp.where(swapped, left[part, row : row + 128], right[part, row : row + 128]) * mask for part in (0, 1)
+    )
+
+
+def mid_block(block, mask, b_s, got):
+    rows = at(block * 128, 128)
+    return tuple(b_s[part, rows] * mask - got[:, part * 128 : part * 128 + 128] for part in (0, 1))
+
+
+def leaf_block(j, supernode, mask, g, got):
+    rows = at(j * 512 + supernode * 128, 128)
+    return tuple(g[part, rows] * mask - got[:, part * 128 : part * 128 + 128] for part in (0, 1))
+
+
+def make_head_kernel(planes):
+    def kernel(
+        mask_ref, mine, other, g, rhs_h, rhs_l, x_h, x_l, t_h, t_l, tl_h, tl_l,
+        b_s, am_s, ra_h, ra_l, lhs_h, lhs_l,
+    ):
+        plane, pair, swapped = places(planes)
+        mid_blocks(planes, mine, other, b_s, am_s, ra_h, ra_l)
+        masks = [mask_ref[pl.ds(pair * 2 + e, 1), :] for e in (0, 1)]
+        for e in (0, 1):
+            re, im = top_block(e, swapped, mine, other, 0, masks[e])
+            put_pair(lhs_h, lhs_l, e * 128, 256, re, im)
+            put_block(x_h.at[0], x_l.at[0], t_h, t_l, 0, e, re, im)
+        got = mm3(lhs_h[:, 256:512], lhs_l[:, 256:512], ra_h[...], ra_l[...])
+        for e in (0, 1):
+            re, im = mid_block(pair * 2 + e, masks[e], b_s, got[e * 128 : e * 128 + 128])
+            put_pair(lhs_h, lhs_l, e * 128, 0, re, im)
+            put_block(x_h.at[1], x_l.at[1], t_h, t_l, 256, e, re, im)
+        for j in range(x_h.shape[0] - 2):
+            got = mm3(lhs_h[...], lhs_l[...], rhs_h[j], rhs_l[j])
+            for e in (0, 1):
+                supernode = plane ^ (pair * 2 + e)
+                re, im = leaf_block(j, supernode, masks[e], g, got[e * 128 : e * 128 + 128])
+                put_block(x_h.at[2 + j], x_l.at[2 + j], tl_h.at[j], tl_l.at[j], 0, e, re, im)
+
+    return kernel
+
+
+def head(planes, masks, mine, other, prepared):
+    g, _, rhs_h, rhs_l, _, _ = prepared
+    leaves = g.shape[1] // 512
+    v = pltpu.VMEM
+    pair = lambda *shape: [v(shape, BF16)] * 2
+    shapes = [(leaves + 2, 512, 256)] * 2 + [(512, 256)] * 2 + [(leaves, 256, 256)] * 2
+    return pl.pallas_call(
+        make_head_kernel(planes),
+        out_shape=tuple(jax.ShapeDtypeStruct(s, BF16) for s in shapes),
+        in_specs=[VMEM] * 6,
+        out_specs=(VMEM,) * 6,
+        scratch_shapes=[
+            v((2, 512, 128), F32), v((2, 128, 128), F32), *pair(256, 256), *pair(256, 512),
+        ],
+        compiler_params=pltpu.CompilerParams(vmem_limit_bytes=16 << 20),
+        cost_estimate=pl.CostEstimate(flops=1_000_000, bytes_accessed=1_000, transcendentals=0),
+        name="head",
+    )(masks, mine, other, g, rhs_h, rhs_l)
+
+
+def pick(near, r, first, second, j):
+    rows = slice(r % 2 * 256, r % 2 * 256 + 256)
+    if r < 2:
+        return jnp.where(near, first[j, rows], second[j, rows])
+    return jnp.where(near, second[j, rows], first[j, rows])
+
+
+def own_columns(j, row_h, row_l, col_h, col_l, xs, out, first, planes):
+    near = places(planes)[1] == 0
+    xa_h, xa_l, xb_h, xb_l = xs
+    xh = jnp.concatenate([xa_h[j], xb_h[j]], axis=0)
+    xl = jnp.concatenate([xa_l[j], xb_l[j]], axis=0)
+    out[j - first, 0:128] = mm3(row_h[...], row_l[...], xh, xl)
+    out[j - first, 128:512] = mm3(
+        col_h[...], col_l[...], pick(near, 0, xa_h, xb_h, j), pick(near, 0, xa_l, xb_l, j)
+    )
 
 
 def make_front_kernel(planes, leaves):
     def kernel(
-        mask_ref, mine, other, both, both_other, g_s, li_s, rhs_h, rhs_l, auxl_h, auxl_l,
-        x_h, x_l, tt_h, tt_l, tl_h, tl_l, base_top, base_leaf, row_h, row_l, col_h, col_l, c_top,
-        l_s, b_s, t0_s, am_s, d_s, own,
+        mask_ref, mine, other, both, both_other, g_s, li_s, rhs_h, rhs_l, auxl_h, auxl_l, xa_h, xa_l,
+        x_h, x_l, t_h, t_l, tl_h, tl_l, base_top, base_leaf, row_h, row_l, col_h, col_l, c_top,
+        b_s, t0_s, am_s, d_s, own,
         lhs_h, lhs_l, ra_h, ra_l, rq_h, rq_l, aux_h, aux_l, rrs_h, rrs_l,
     ):
         device = lax.axis_index("row")
         plane = own_plane(device, planes)
         quarter = device % 4
         half = device % 2
-        def rel(supernode):
-            return at((supernode ^ plane) * 128, 128)
-
         for k, (ref, row) in enumerate(((mine, 0), (other, 0), (both, 192), (both_other, 192))):
             q = quarter ^ k
-            l_s[:, rel(q), :] = ref[:, row : row + 128, :]
             t0_s[:, at(q * 32, 32), :] = ref[:, row + 128 : row + 160, :]
             for n in range(4):
                 own[:, at(q * 32, 32), n * 128 : n * 128 + 128] = (
                     ref[:, row + 160 + n * 32 : row + 192 + n * 32, :]
                 )
         for k, ref in enumerate((mine, other)):
-            h = half ^ k
-            for n in (0, 1):
-                b_s[:, rel(h * 2 + n), :] = ref[:, 288 + n * 128 : 416 + n * 128, :]
-            am_s[:, at(h * 64, 64), :] = ref[:, 544:608, :]
-            d_s[:, at(h * 64, 64), :] = ref[:, 608:672, :]
-        masks = [mask_ref[r : r + 1, :] for r in range(4)]
-
-        def put_x(j, r, re, im):
-            put_rhs(x_h.at[j], x_l.at[j], r * 256, re, im)
-
-        put_rhs(ra_h, ra_l, 0, am_s[0], am_s[1])
-        for r in range(4):
-            rows = slice(r * 128, r * 128 + 128)
-            re, im = l_s[0, rows] * masks[r], l_s[1, rows] * masks[r]
-            put_pair(lhs_h, lhs_l, r * 128, 256, re, im)
-            put_x(0, r, re, im)
-            put_transposed(tt_h, tt_l, 0, r, re, im)
-        put_pair(lhs_h, lhs_l, 640, 256, t0_s[0], t0_s[1])
+            d_s[:, at((half ^ k) * 64, 64), :] = ref[:, 608:672, :]
+        mid_blocks(planes, mine, other, b_s, am_s, ra_h, ra_l)
+        _, pair, swapped = places(planes)
+        pair = 1 - pair
+        masks = [mask_ref[pl.ds(pair * 2 + e, 1), :] for e in (0, 1)]
+        for e in (0, 1):
+            re, im = top_block(e, swapped, both, both_other, 192, masks[e])
+            put_pair(lhs_h, lhs_l, e * 128, 256, re, im)
+            put_block(x_h.at[0], x_l.at[0], t_h, t_l, 0, e, re, im)
+        put_pair(lhs_h, lhs_l, 384, 256, t0_s[0], t0_s[1])
         ah, al = ra_h[...], ra_l[...]
-        got = mm3(lhs_h[0:512, 256:512], lhs_l[0:512, 256:512], ah, al)
-        for r in range(4):
-            rows = slice(r * 128, r * 128 + 128)
-            re = b_s[0, rows] * masks[r] - got[rows, 0:128]
-            im = b_s[1, rows] * masks[r] - got[rows, 128:256]
-            put_pair(lhs_h, lhs_l, r * 128, 0, re, im)
-            put_x(1, r, re, im)
-            put_transposed(tt_h, tt_l, 256, r, re, im)
-        got = mm3(lhs_h[640:768, 256:512], lhs_l[640:768, 256:512], ah, al)
+        got = mm3(lhs_h[0:256, 256:512], lhs_l[0:256, 256:512], ah, al)
+        for e in (0, 1):
+            re, im = mid_block(pair * 2 + e, masks[e], b_s, got[e * 128 : e * 128 + 128])
+            put_pair(lhs_h, lhs_l, e * 128, 0, re, im)
+            put_block(x_h.at[1], x_l.at[1], t_h, t_l, 256, e, re, im)
+        got = mm3(lhs_h[384:512, 256:512], lhs_l[384:512, 256:512], ah, al)
         q_r, q_i = -got[:, 0:128], -got[:, 128:256]
-        put_pair(lhs_h, lhs_l, 640, 0, q_r, q_i)
-        put_pair(lhs_h, lhs_l, 512, 256, q_r.T, q_i.T)
+        put_pair(lhs_h, lhs_l, 384, 0, q_r, q_i)
+        put_pair(lhs_h, lhs_l, 256, 256, q_r.T, q_i.T)
         put_rhs(rq_h, rq_l, 0, q_r, q_i)
         put_pair(aux_h, aux_l, 0, 0, am_s[0].T, am_s[1].T)
         got = mm3(aux_h[...], aux_l[...], rq_h[...], rq_l[...])
         d_r, d_i = d_s[0] - got[:, 0:128], d_s[1] - got[:, 128:256]
-        put_pair(lhs_h, lhs_l, 512, 0, d_r, d_i)
+        put_pair(lhs_h, lhs_l, 256, 0, d_r, d_i)
         base_top[0] = t0_s[...]
         base_top[1, 0] = q_r
         base_top[1, 1] = q_i
         base_top[2, 0] = d_r
         base_top[2, 1] = d_i
-
-        for r in range(4):
+        for n in range(4):
+            cols = at((plane ^ (2 - pair * 2) ^ n) * 128, 128)
+            put_pair(row_h, row_l, 0, n * 256, own[0, :, cols], own[1, :, cols])
+        for r in range(1, 4):
             cols = at((plane ^ r) * 128, 128)
-            re, im = own[0, :, cols], own[1, :, cols]
-            put_pair(row_h, row_l, 0, r * 256, re, im)
-            if r:
-                put_pair(col_h, col_l, (r - 1) * 128, 0, re.T, im.T)
+            put_pair(col_h, col_l, (r - 1) * 128, 0, own[0, :, cols].T, own[1, :, cols].T)
         for j in (0, 1):
-            own_columns(j, row_h, row_l, col_h, col_l, x_h, x_l, c_top)
+            own_columns(j, row_h, row_l, col_h, col_l, (xa_h, xa_l, x_h, x_l), c_top, 0, planes)
         for j in range(leaves):
             got = mm3(lhs_h[...], lhs_l[...], rhs_h[j], rhs_l[j])
-            for r in range(4):
-                rows = slice(r * 128, r * 128 + 128)
-                mine = at(j * 512 + (plane ^ r) * 128, 128)
-                re = g_s[0, mine] * masks[r] - got[rows, 0:128]
-                im = g_s[1, mine] * masks[r] - got[rows, 128:256]
-                put_x(2 + j, r, re, im)
-                put_transposed(tl_h.at[j], tl_l.at[j], 0, r, re, im)
-            r_r, r_i = -got[512:640, 0:128], -got[512:640, 128:256]
-            s_r, s_i = -got[640:768, 0:128], -got[640:768, 128:256]
+            for e in (0, 1):
+                re, im = leaf_block(j, plane ^ (pair * 2 + e), masks[e], g_s, got[e * 128 : e * 128 + 128])
+                put_block(x_h.at[2 + j], x_l.at[2 + j], tl_h.at[j], tl_l.at[j], 0, e, re, im)
+            r_r, r_i = -got[256:384, 0:128], -got[256:384, 128:256]
+            s_r, s_i = -got[384:512, 0:128], -got[384:512, 128:256]
             put_rhs(rrs_h.at[j], rrs_l.at[j], 0, r_r, r_i)
             put_rhs(rrs_h.at[j], rrs_l.at[j], 256, s_r, s_i)
             base_leaf[j, 0, 0] = s_r
@@ -256,21 +365,21 @@
             base_leaf[j, 1, 0] = r_r
             base_leaf[j, 1, 1] = r_i
         for j in range(leaves):
-            mine = slice(j * 128, j * 128 + 128)
+            mine_rows = slice(j * 128, j * 128 + 128)
             got = mm3(auxl_h[j], auxl_l[j], rrs_h[j], rrs_l[j])
-            base_leaf[j, 2, 0] = li_s[0, mine] - got[:, 0:128]
-            base_leaf[j, 2, 1] = li_s[1, mine] - got[:, 128:256]
+            base_leaf[j, 2, 0] = li_s[0, mine_rows] - got[:, 0:128]
+            base_leaf[j, 2, 1] = li_s[1, mine_rows] - got[:, 128:256]
 
     return kernel
 
 
-def front(planes, masks, pieces, prepared):
+def front(planes, masks, pieces, prepared, heads):
     leaves = prepared[0].shape[1] // 512
     n = leaves + 2
     v = pltpu.VMEM
     out = [
-        ((n, 1024, 256), BF16), ((n, 1024, 256), BF16), ((512, 512), BF16), ((512, 512), BF16),
-        ((leaves, 256, 512), BF16), ((leaves, 256, 512), BF16),
+        ((n, 512, 256), BF16), ((n, 512, 256), BF16), ((512, 256), BF16), ((512, 256), BF16),
+        ((leaves, 256, 256), BF16), ((leaves, 256, 256), BF16),
         ((3, 2, 128, 128), F32), ((leaves, 3, 2, 128, 128), F32),
         ((128, 1024), BF16), ((128, 1024), BF16), ((384, 256), BF16), ((384, 256), BF16),
         ((2, 512, 256), F32),
@@ -279,41 +388,40 @@
     return pl.pallas_call(
         make_front_kernel(planes, leaves),
         out_shape=tuple(jax.ShapeDtypeStruct(s, d) for s, d in out),
-        in_specs=[VMEM] * 11,
+        in_specs=[VMEM] * 13,
         out_specs=(VMEM,) * len(out),
         scratch_shapes=[
-            v((2, 512, 128), F32), v((2, 512, 128), F32),
+            v((2, 512, 128), F32),
             v((2, 128, 128), F32), v((2, 128, 128), F32), v((2, 128, 128), F32),
-            v((2, 128, 512), F32), *pair(768, 512), *pair(256, 256), *pair(256, 256), *pair(128, 256),
+            v((2, 128, 512), F32), *pair(512, 512), *pair(256, 256), *pair(256, 256), *pair(128, 256),
             *pair(leaves, 512, 256),
         ],
-        compiler_params=pltpu.CompilerParams(vmem_limit_bytes=24 << 20),
+        compiler_params=pltpu.CompilerParams(vmem_limit_bytes=16 << 20),
         cost_estimate=pl.CostEstimate(flops=1_000_000, bytes_accessed=1_000, transcendentals=0),
         name="front",
-    )(masks, *pieces, *prepared)
-
-
-def own_kernel(row_h, row_l, col_h, col_l, x_h, x_l, c_leaf):
-    for j in range(2, x_h.shape[0]):
-        own_columns(j, row_h, row_l, col_h, col_l, x_h, x_l, c_leaf, 2)
-
-
-def own_product(row_h, row_l, col_h, col_l, x_h, x_l):
-    return pl.pallas_call(
-        own_kernel,
-        out_shape=jax.ShapeDtypeStruct((x_h.shape[0] - 2, 512, 256), F32),
-        in_specs=[VMEM] * 6,
+    )(masks, *pieces, *prepared, *heads[:2])
+
+
+def own_product(planes, row_h, row_l, col_h, col_l, *xs):
+    def kernel(row_h, row_l, col_h, col_l, xa_h, xa_l, xb_h, xb_l, c_leaf):
+        for j in range(2, xa_h.shape[0]):
+            own_columns(j, row_h, row_l, col_h, col_l, (xa_h, xa_l, xb_h, xb_l), c_leaf, 2, planes)
+
+    return pl.pallas_call(
+        kernel,
+        out_shape=jax.ShapeDtypeStruct((xs[0].shape[0] - 2, 512, 256), F32),
+        in_specs=[VMEM] * 8,
         out_specs=VMEM,
         compiler_params=pltpu.CompilerParams(vmem_limit_bytes=12 << 20),
         cost_estimate=pl.CostEstimate(flops=1_000_000, bytes_accessed=1_000, transcendentals=0),
         name="own_product",
-    )(row_h, row_l, col_h, col_l, x_h, x_l)
+    )(row_h, row_l, col_h, col_l, *xs)
 
 
 def make_back_kernel(planes, leaves):
     def kernel(
-        mask_ref, b0, b1, b2, b3,
-        x_h, x_l, tt_h, tt_l, tl_h, tl_l, base_top, base_leaf, c_top, c_leaf,
+        mask_ref, b0, b1, b2, b3, xa_h, xa_l, ta_h, ta_l, tla_h, tla_l,
+        xb_h, xb_l, tb_h, tb_l, tlb_h, tlb_l, base_top, base_leaf, c_top, c_leaf,
         col_top, diag_top, col_mid, cross_mid, diag_mid, col_leaf, cross_c, cross_e, diag_leaf,
         blocks, a_h, a_l, cb_h, cb_l, c_s, d_s, e_s, f_s, top_s, mid_s, sem,
     ):
@@ -330,17 +438,20 @@
             return copy
 
         masks = [-mask_ref[r : r + 1, :] for r in range(4)]
+        near = places(planes)[1] == 0
         for k, ref in enumerate((b0, b1, b2, b3)):
             for n in range(6):
                 blocks[n, :, at((quarter ^ k) * 32, 32), :] = ref[:, n * 32 : n * 32 + 32, :]
-        for n, (row, col) in enumerate(((1, 1), (1, 2), (1, 3), (2, 2), (2, 3), (3, 3))):
+        for n, (row, col) in enumerate(((1, 1), (1, 2), (1, 3), (2, 2), (3, 3), (3, 2))):
             re, im = blocks[n, 0], blocks[n, 1]
             put_pair(a_h, a_l, row * 128 - 128, col * 256 - 256, re, im)
             if row != col:
                 put_pair(a_h, a_l, col * 128 - 128, row * 256 - 256, re.T, im.T)
 
         def columns(j, out):
-            got = mm3(a_h[...], a_l[...], x_h[j, 256:1024], x_l[j, 256:1024])
+            xh = jnp.concatenate([pick(near, r, xa_h, xb_h, j) for r in (1, 2, 3)], axis=0)
+            xl = jnp.concatenate([pick(near, r, xa_l, xb_l, j) for r in (1, 2, 3)], axis=0)
+            got = mm3(a_h[...], a_l[...], xh, xl)
             for r in range(4):
                 rows = slice(r * 128, r * 128 + 128)
                 place = at((plane ^ r) * 128, 128)
@@ -363,9 +474,14 @@
                 outs.append((g[0:128, 0:128] - g[128:256, 128:256], g[0:128, 128:256] + g[128:256, 0:128]))
             return outs
 
+        def across(first, second):
+            return jnp.concatenate([jnp.where(near, first, second), jnp.where(near, second, first)], axis=1)
+
+        tt_h, tt_l = across(ta_h[...], tb_h[...]), across(ta_l[...], tb_l[...])
+
         def leaf_tail(j):
-            th = jnp.concatenate([tt_h[...], tl_h[j]], axis=0)
-            tl = jnp.concatenate([tt_l[...], tl_l[j]], axis=0)
+            th = jnp.concatenate([tt_h, across(tla_h[j], tlb_h[j])], axis=0)
+            tl = jnp.concatenate([tt_l, across(tla_l[j], tlb_l[j])], axis=0)
             zs = against(2 + j, th, tl)
             for n, (z, out) in enumerate(zip(zs, (e_s, d_s, f_s))):
                 for part in (0, 1):
@@ -384,7 +500,7 @@
         move(c_s.at[0, :, at(quarter * 128, 128), :], col_top)
         for j in range(leaves):
             leaf_tail(j)
-        zs = against(1, tt_h[...], tt_l[...])
+        zs = against(1, tt_h, tt_l)
         for n in (0, 1):
             for part in (0, 1):
                 mid_s[n, part] = base_top[1 + n, part] - zs[n][part]
@@ -431,7 +547,7 @@
     root = []
     for k in range(4):
         pieces = []
-        for row, col in ((1, 1), (1, 2), (1, 3), (2, 2), (2, 3), (3, 3)):
+        for row, col in ((1, 1), (1, 2), (1, 3), (2, 2), (3, 3), (3, 2)):
             block = full[:, row * 128 : row * 128 + 128, col * 128 : col * 128 + 128]
             pieces.append(lax.dynamic_slice_in_dim(block, (quarter ^ k) * 32, 32, 1))
         root.append(jnp.concatenate(pieces, axis=1))
@@ -450,9 +566,11 @@
             pattern, ainv_root, panel_top, inv_top, panel_mid, link_mid, inv_mid
         )
         got = [swap(x, 4 * k) for k, x in zip((1, 2, 3), sent)]
-        *got, _ = lax.optimization_barrier((*got, *prepared))[:4]
-        near, both = join(*got, swap(top, 2))
-        far = swap(near, 2)
+        other = swap(mine, 1)
+        heads = head(planes, masks, mine, other, prepared)
+        *got, _ = lax.optimization_barrier((*got, heads))
+        lead, rest, both = join(*got, swap(top, 2))
+        far = [swap(lead, 4), swap(rest, 2)]
     else:
         node = lax.dynamic_index_in_dim(pattern, lax.axis_index("row") // 4, 0, keepdims=False)
         masks = jnp.broadcast_to(jnp.pad(node.astype(F32), (0, 4))[:, None], (8, 128))
@@ -461,13 +579,16 @@
         top = jnp.concatenate([panel_top, inv_top, *own], axis=1)
         mine = jnp.concatenate([top, panel_mid, link_mid, inv_mid], axis=1)
         both = jnp.concatenate([root[0], swap(top, 2)], axis=1)
-    pieces = [mine, swap(mine, 1), both, swap(both, 1)]
-    firsts = front(planes, masks, pieces, prepared)
+        other = swap(mine, 1)
+        heads = head(planes, masks, mine, other, prepared)
+    pieces = [mine, other, both, swap(both, 1)]
+    firsts = front(planes, masks, pieces, prepared, heads)
     if planes:
-        far, *firsts = lax.optimization_barrier((far, *firsts))
+        *far, firsts = lax.optimization_barrier((*far, firsts))
+        far = stack(*far)
         root = [both, pieces[3], far, swap(far, 1)]
-    c_leaf = own_product(*firsts[8:12], *firsts[:2])
-    return back(planes, masks, root, [*firsts[:8], firsts[12], c_leaf], leaves)
+    c_leaf = own_product(planes, *firsts[8:12], *heads[:2], *firsts[:2])
+    return back(planes, masks, root, [*heads, *firsts[:8], firsts[12], c_leaf], leaves)
 
 
 def solution(mesh):

time: 30.1 us -> 27.8 us (0.924)
  waiting for transfers between devices: 6.16 us -> 2.52 us
  starting transfers between devices: 8.07 us -> 9.09 us
    ppermute x8 -> x9, waiting for transfers between devices: 6.16 us -> 2.52 us  [swap(): lax.ppermute(x, 'row', [(i, i ^ apart) for i in range(lax.axis_size('row'...]
    pallas_call x2 -> x4, Pallas kernels: 1.29 us -> 2.67 us  [the longest x1 1.34 us: head(): pl.pallas_call(make_head_kernel(planes), out_shape=tuple((jax.ShapeDtypeS...]
    ppermute x8 -> x9, starting transfers between devices: 8.07 us -> 9.09 us  [swap(): lax.ppermute(x, 'row', [(i, i ^ apart) for i in range(lax.axis_size('row'...]
    pallas_call x1, Pallas kernels: 4.52 us -> 3.54 us  [front(): pl.pallas_call(make_front_kernel(planes, leaves), out_shape=tuple((jax.Sh...]
  transfers between devices with their start and end apart: 8 -> 9, of which waited for: 4 -> 2; matrix products, arithmetic and copies ran while one was open for 0% -> 0% of each run, Pallas kernels for 25% -> 28%
where the time goes in v3:
time: 27.8 us; the launch traced here: 27.7 us
  Pallas kernels  15.3 us (55%)
  starting transfers between devices  9.09 us (33%)
  waiting for transfers between devices  2.52 us (9%)
  between operations  0.74 us (3%)
    ppermute x9, starting transfers between devices, swap(): lax.ppermute(x, 'row', [(i, i ^ apart) for i in range(lax.axis_size('row'...  9.09 us
    pallas_call x1, Pallas kernels, back(): pl.pallas_call(make_back_kernel(planes, leaves), out_shape=tuple((jax.Sha...  6.18 us
    pallas_call x1, Pallas kernels, front(): pl.pallas_call(make_front_kernel(planes, leaves), out_shape=tuple((jax.Sh...  3.54 us
    ppermute x9, waiting for transfers between devices, swap(): lax.ppermute(x, 'row', [(i, i ^ apart) for i in range(lax.axis_size('row'...  2.52 us
    pallas_call x1, Pallas kernels, prep(): pl.pallas_call(make_prep_kernel(leaves), out_shape=tuple((jax.ShapeDtypeS...  1.74 us
    pallas_call x1, Pallas kernels, head(): pl.pallas_call(make_head_kernel(planes), out_shape=tuple((jax.ShapeDtypeS...  1.34 us
    pallas_call x1, Pallas kernels, own_product(): pl.pallas_call(kernel, out_shape=jax.ShapeDtypeStruct((xs[0].shape[0] - 2...  1.27 us
    pallas_call x1, Pallas kernels, pack(): pl.pallas_call(pack_kernel, out_shape=tuple((jax.ShapeDtypeStruct(s, F32)...  1.17 us
  transfers between devices with their start and end apart: 9, of which 2 were waited for; matrix products, arithmetic and copies ran while one was open for 0% of the time, Pallas kernels for 28%

profile of v3, /device:TPU:0, one launch (start us, length us, event | category | flops | bytes accessed | tf_op | source)
XLA Modules:
  0.0 27.7 jit_solution(10944057297900133336)
XLA Ops:
  0.6 1.2 %pack_panels.1 = (f32[2,288,128]{2,1,0:T(8,128)S(1)}, f32[2,672,128]{2,1,0:T(8,128)S(1)}, f32[8,128]{1,0:T(8,128)S(1)}, f32[2,96,128]{2,1,0:T(8,128)S(1)}, f32[2...) custom-call(s32[4,4]{1,0:T(4,128)} %pat.1, f32[2,32,512]{2,1,0:T(8,128)} %a_hbm.1, f32[2,128,128]{2,1,0:T(8,128)} %t_hbm.1, ...), custom_call_target="tpu_custom_call" | custom-call | flops 1000000 | bytes 1000 | tf_op jit(solution)/shard_map/pack_panels/pallas_call | solution.py:74
  1.8 0.5 %collective-permute-start.3 = (f32[2,672,128]{2,1,0:T(8,128)S(1)}, f32[2,672,128]{2,1,0:T(8,128)S(1)}, u32[]{:S(2)}, u32[]{:S(2)}) collective-permute-start(f32[2,672,128]{2,1,0:T(8,128)S(1)} %get-tuple-element.65.mine), channel_id=1, source_target_pairs={{0,1},{1,0},{2,3},{3,2},{4,5},{5,4},{6,7},{7,6},{8,9},{9,8},{10,11... | collective-permute-start | bytes 2064392 | tf_op jit(solution)/shard_map/ppermute | solution.py:15
  2.3 2.6 %collective-permute-start.4 = (f32[2,288,128]{2,1,0:T(8,128)S(1)}, f32[2,288,128]{2,1,0:T(8,128)S(1)}, u32[]{:S(2)}, u32[]{:S(2)}) collective-permute-start(f32[2,288,128]{2,1,0:T(8,128)S(1)} %get-tuple-element.78), channel_id=1, source_target_pairs={{0,2},{1,3},{2,0},{3,1},{4,6},{5,7},{6,4},{7,5},{8,10},{9,11},{10,... | collective-permute-start | bytes 884744 | tf_op jit(solution)/shard_map/ppermute | solution.py:15
  4.9 1.6 %collective-permute-start = (f32[2,96,128]{2,1,0:T(8,128)S(1)}, f32[2,96,128]{2,1,0:T(8,128)S(1)}, u32[]{:S(2)}, u32[]{:S(2)}) collective-permute-start(f32[2,96,128]{2,1,0:T(8,128)S(1)} %get-tuple-element.62), channel_id=1, source_target_pairs={{0,4},{1,5},{2,6},{3,7},{4,0},{5,1},{6,2},{7,3},{8,12},{9,13},{10,... | collective-permute-start | bytes 294920 | tf_op jit(solution)/shard_map/ppermute | solution.py:15
  6.5 2.5 %collective-permute-start.2 = (f32[2,64,128]{2,1,0:T(8,128)S(1)}, f32[2,64,128]{2,1,0:T(8,128)S(1)}, u32[]{:S(2)}, u32[]{:S(2)}) collective-permute-start(f32[2,64,128]{2,1,0:T(8,128)S(1)} %get-tuple-element.64), channel_id=1, source_target_pairs={{0,12},{1,13},{2,14},{3,15},{4,8},{5,9},{6,10},{7,11},{8,4},{9,5},... | collective-permute-start | bytes 196616 | tf_op jit(solution)/shard_map/ppermute | solution.py:15
  9.0 0.1 collective-permute-start.1
  9.1 1.7 %prep.1 = (f32[2,1536,128]{2,1,0:T(8,128)S(1)}, f32[2,384,128]{2,1,0:T(8,128)S(1)}, bf16[3,512,256]{2,1,0:T(8,128)(2,1)S(1)}, bf16[3,512,256]{2,1,0:T(8,128)(2,1...) custom-call(f32[2,1536,128]{2,1,0:T(8,128)} %panel.1, f32[2,384,128]{2,1,0:T(8,128)} %link_c.1, ...), custom_call_target="tpu_custom_call" | custom-call | flops 1000000 | bytes 1000 | tf_op jit(solution)/shard_map/prep/pallas_call | solution.py:179
  10.9 0.0 collective-permute-done.3.other
  10.9 1.3 %head.1 = (bf16[5,512,256]{2,1,0:T(8,128)(2,1)S(1)}, bf16[5,512,256]{2,1,0:T(8,128)(2,1)S(1)}, bf16[512,256]{1,0:T(8,128)(2,1)S(1)}, bf16[512,256]{1,0:T(8,128)(...) custom-call(f32[8,128]{1,0:T(8,128)S(1)} %get-tuple-element.61.mask_ref, ...), custom_call_target="tpu_custom_call" | custom-call | flops 1000000 | bytes 1000 | tf_op jit(solution)/shard_map/head/pallas_call | solution.py:265
  12.2 2.2 %collective-permute-done.1.z2 = f32[2,32,128]{2,1,0:T(8,128)S(1)} collective-permute-done((f32[2,32,128]{2,1,0:T(8,128)S(1)}, f32[2,32,128]{2,1,0:T(8,128)S(1)}, u32[]{:S(2)}, u32[]{:S(2)}) %collective-permute-start.1) | collective-permute-done | bytes 32800 | tf_op jit(solution)/shard_map/ppermute | solution.py:15
  14.4 0.0 collective-permute-done.2.z3
  14.4 0.0 collective-permute-done.z1
  14.4 0.0 collective-permute-done.4.far_top
  14.4 0.1 collective-permute-start.5
  14.5 0.3 %collective-permute-start.6 = (f32[2,96,128]{2,1,0:T(8,128)S(1)}, f32[2,96,128]{2,1,0:T(8,128)S(1)}, u32[]{:S(2)}, u32[]{:S(2)}) collective-permute-start(f32[2,96,128]{2,1,0:T(8,128)S(1)} %get-tuple-element.80), channel_id=1, source_target_pairs={{0,4},{1,5},{2,6},{3,7},{4,0},{5,1},{6,2},{7,3},{8,12},{9,13},{10,... | collective-permute-start | bytes 294920 | tf_op jit(solution)/shard_map/ppermute | solution.py:15
  14.8 1.3 %collective-permute-start.7 = (f32[2,96,128]{2,1,0:T(8,128)S(1)}, f32[2,96,128]{2,1,0:T(8,128)S(1)}, u32[]{:S(2)}, u32[]{:S(2)}) collective-permute-start(f32[2,96,128]{2,1,0:T(8,128)S(1)} %get-tuple-element.81), channel_id=1, source_target_pairs={{0,2},{1,3},{2,0},{3,1},{4,6},{5,7},{6,4},{7,5},{8,10},{9,11},{10,... | collective-permute-start | bytes 294920 | tf_op jit(solution)/shard_map/ppermute | solution.py:15
  16.1 0.3 %collective-permute-done.5.both_other.b1 = f32[2,480,128]{2,1,0:T(8,128)S(1)} collective-permute-done((f32[2,480,128]{2,1,0:T(8,128)S(1)}, f32[2,480,128]{2,1,0:T(8,128)S(1)}, u32[]{:S(2)}, u32[]{:S(2)}) %collective-permute-start.5) | collective-permute-done | bytes 491552 | tf_op jit(solution)/shard_map/ppermute | solution.py:15
  16.4 3.5 %front.1 = (bf16[5,512,256]{2,1,0:T(8,128)(2,1)S(1)}, bf16[5,512,256]{2,1,0:T(8,128)(2,1)S(1)}, bf16[512,256]{1,0:T(8,128)(2,1)S(1)}, bf16[512,256]{1,0:T(8,128)...) custom-call(f32[8,128]{1,0:T(8,128)S(1)} %get-tuple-element.61.mask_, ...), custom_call_target="tpu_custom_call" | custom-call | flops 1000000 | bytes 1000 | tf_op jit(solution)/shard_map/front/pallas_call | solution.py:388
  19.9 0.0 collective-permute-done.6.upper
  19.9 0.0 collective-permute-done.7.lower
  20.0 0.2 collective-permute-start.8
  20.2 1.3 %own_product.1.c_leaf = f32[3,512,256]{2,1,0:T(8,128)S(1)} custom-call(bf16[128,1024]{1,0:T(8,128)(2,1)S(1)} %get-tuple-element.109.row_h, bf16[128,1024]{1,0:T(8,128)(2,1)S(1)} %get-tuple-element.110.row_l, bf16[384,256]{1,0:T(8,128)(2,1)S(1)} %get-tuple-element.111.col_h, bf16[384,256]{1,0:T(8,128)(2,1)S(1)} %get-tuple-element.112.col_l, ...), custom_call_target="tpu_custom_call" | custom-call | flops 1000000 | bytes 1000 | tf_op jit(solution)/shard_map/own_product/pallas_call | solution.py:410
  21.4 0.0 collective-permute-done.8.b3
  21.5 6.2 %back.1 = (f32[2,128,128]{2,1,0:T(8,128)}, f32[2,32,128]{2,1,0:T(8,128)}, f32[2,256,128]{2,1,0:T(8,128)}, f32[2,64,128]{2,1,0:T(8,128)}, f32[2,64,128]{2,1,0:T(8...) custom-call(f32[8,128]{1,0:T(8,128)S(1)} %get-tuple-element.61.mask_r, ...), custom_call_target="tpu_custom_call" | custom-call | flops 8000000000 | bytes 12000000 | tf_op jit(solution)/shard_map/back/pallas_call | solution.py:525
  (2 shorter events, 0.1 us)
Async XLA Ops:
  1.8 9.0 %collective-permute-start.3 = (f32[2,672,128]{2,1,0:T(8,128)S(1)}, f32[2,672,128]{2,1,0:T(8,128)S(1)}, u32[]{:S(2)}, u32[]{:S(2)}) collective-permute-start(f32[2,672,128]{2,1,0:T(8,128)S(1)} %get-tuple-element.65.mine), channel_id=1, source_target_pairs={{0,1},{1,0},{2,3},{3,2},{4,5},{5,4},{6,7},{7,6},{8,9},{9,8},{10,11... | collective-permute-start | bytes 2064392 | tf_op jit(solution)/shard_map/ppermute | solution.py:15
  2.3 12.0 %collective-permute-start.4 = (f32[2,288,128]{2,1,0:T(8,128)S(1)}, f32[2,288,128]{2,1,0:T(8,128)S(1)}, u32[]{:S(2)}, u32[]{:S(2)}) collective-permute-start(f32[2,288,128]{2,1,0:T(8,128)S(1)} %get-tuple-element.78), channel_id=1, source_target_pairs={{0,2},{1,3},{2,0},{3,1},{4,6},{5,7},{6,4},{7,5},{8,10},{9,11},{10,... | collective-permute-start | bytes 884744 | tf_op jit(solution)/shard_map/ppermute | solution.py:15
  4.9 9.4 %collective-permute-start = (f32[2,96,128]{2,1,0:T(8,128)S(1)}, f32[2,96,128]{2,1,0:T(8,128)S(1)}, u32[]{:S(2)}, u32[]{:S(2)}) collective-permute-start(f32[2,96,128]{2,1,0:T(8,128)S(1)} %get-tuple-element.62), channel_id=1, source_target_pairs={{0,4},{1,5},{2,6},{3,7},{4,0},{5,1},{6,2},{7,3},{8,12},{9,13},{10,... | collective-permute-start | bytes 294920 | tf_op jit(solution)/shard_map/ppermute | solution.py:15
  6.5 7.9 %collective-permute-start.2 = (f32[2,64,128]{2,1,0:T(8,128)S(1)}, f32[2,64,128]{2,1,0:T(8,128)S(1)}, u32[]{:S(2)}, u32[]{:S(2)}) collective-permute-start(f32[2,64,128]{2,1,0:T(8,128)S(1)} %get-tuple-element.64), channel_id=1, source_target_pairs={{0,12},{1,13},{2,14},{3,15},{4,8},{5,9},{6,10},{7,11},{8,4},{9,5},... | collective-permute-start | bytes 196616 | tf_op jit(solution)/shard_map/ppermute | solution.py:15
  9.0 5.4 %collective-permute-start.1 = (f32[2,32,128]{2,1,0:T(8,128)S(1)}, f32[2,32,128]{2,1,0:T(8,128)S(1)}, u32[]{:S(2)}, u32[]{:S(2)}) collective-permute-start(f32[2,32,128]{2,1,0:T(8,128)S(1)} %get-tuple-element.63), channel_id=1, source_target_pairs={{0,8},{1,9},{2,10},{3,11},{4,12},{5,13},{6,14},{7,15},{8,0},{9,1},... | collective-permute-start | bytes 98312 | tf_op jit(solution)/shard_map/ppermute | solution.py:15
  14.4 1.9 %collective-permute-start.5 = (f32[2,480,128]{2,1,0:T(8,128)S(1)}, f32[2,480,128]{2,1,0:T(8,128)S(1)}, u32[]{:S(2)}, u32[]{:S(2)}) collective-permute-start(f32[2,480,128]{2,1,0:T(8,128)S(1)} %get-tuple-element.79.both.b0), channel_id=1, source_target_pairs={{0,1},{1,0},{2,3},{3,2},{4,5},{5,4},{6,7},{7,6},{8,9},{9,8},{10,11... | collective-permute-start | bytes 1474568 | tf_op jit(solution)/shard_map/ppermute | solution.py:15
  14.5 5.4 %collective-permute-start.6 = (f32[2,96,128]{2,1,0:T(8,128)S(1)}, f32[2,96,128]{2,1,0:T(8,128)S(1)}, u32[]{:S(2)}, u32[]{:S(2)}) collective-permute-start(f32[2,96,128]{2,1,0:T(8,128)S(1)} %get-tuple-element.80), channel_id=1, source_target_pairs={{0,4},{1,5},{2,6},{3,7},{4,0},{5,1},{6,2},{7,3},{8,12},{9,13},{10,... | collective-permute-start | bytes 294920 | tf_op jit(solution)/shard_map/ppermute | solution.py:15
  14.8 5.1 %collective-permute-start.7 = (f32[2,96,128]{2,1,0:T(8,128)S(1)}, f32[2,96,128]{2,1,0:T(8,128)S(1)}, u32[]{:S(2)}, u32[]{:S(2)}) collective-permute-start(f32[2,96,128]{2,1,0:T(8,128)S(1)} %get-tuple-element.81), channel_id=1, source_target_pairs={{0,2},{1,3},{2,0},{3,1},{4,6},{5,7},{6,4},{7,5},{8,10},{9,11},{10,... | collective-permute-start | bytes 294920 | tf_op jit(solution)/shard_map/ppermute | solution.py:15
  20.0 1.5 %collective-permute-start.8 = (f32[2,192,128]{2,1,0:T(8,128)S(1)}, f32[2,192,128]{2,1,0:T(8,128)S(1)}, u32[]{:S(2)}, u32[]{:S(2)}) collective-permute-start(f32[2,192,128]{2,1,0:T(8,128)S(1)} %stack_root.1.b2), channel_id=1, source_target_pairs={{0,1},{1,0},{2,3},{3,2},{4,5},{5,4},{6,7},{7,6},{8,9},{9,8},{10,11... | collective-permute-start | bytes 589832 | tf_op jit(solution)/shard_map/ppermute | solution.py:15

commit v4 on v3

--- a/solution.py
+++ b/solution.py
@@ -25,7 +25,8 @@
 
 
 def mm3(ah, al, bh, bl):
-    return mm(ah, bh) + (mm(ah, bl) + mm(al, bh))
+    left = jnp.concatenate([ah, ah, al], axis=1)
+    return mm(left, jnp.concatenate([bh, bl, bh], axis=0))
 
 
 def at(start, size):
@@ -231,11 +232,12 @@
 
 def make_head_kernel(planes):
     def kernel(
-        mask_ref, mine, other, g, rhs_h, rhs_l, x_h, x_l, t_h, t_l, tl_h, tl_l,
-        b_s, am_s, ra_h, ra_l, lhs_h, lhs_l,
+        mask_ref, mine, other, g, rhs_h, rhs_l, x_h, x_l, t_h, t_l, tl_h, tl_l, b_s, ra_h, ra_l, at_h, at_l,
+        am_s, lhs_h, lhs_l,
     ):
         plane, pair, swapped = places(planes)
         mid_blocks(planes, mine, other, b_s, am_s, ra_h, ra_l)
+        put_pair(at_h, at_l, 0, 0, am_s[0].T, am_s[1].T)
         masks = [mask_ref[pl.ds(pair * 2 + e, 1), :] for e in (0, 1)]
         for e in (0, 1):
             re, im = top_block(e, swapped, mine, other, 0, masks[e])
@@ -262,14 +264,13 @@
     v = pltpu.VMEM
     pair = lambda *shape: [v(shape, BF16)] * 2
     shapes = [(leaves + 2, 512, 256)] * 2 + [(512, 256)] * 2 + [(leaves, 256, 256)] * 2
+    shapes += [(2, 512, 128), (256, 256), (256, 256), (128, 256), (128, 256)]
     return pl.pallas_call(
         make_head_kernel(planes),
-        out_shape=tuple(jax.ShapeDtypeStruct(s, BF16) for s in shapes),
+        out_shape=tuple(jax.ShapeDtypeStruct(s, BF16 if len(s) != 3 or s[0] != 2 else F32) for s in shapes),
         in_specs=[VMEM] * 6,
-        out_specs=(VMEM,) * 6,
-        scratch_shapes=[
-            v((2, 512, 128), F32), v((2, 128, 128), F32), *pair(256, 256), *pair(256, 512),
-        ],
+        out_specs=(VMEM,) * len(shapes),
+        scratch_shapes=[v((2, 128, 128), F32), *pair(256, 512)],
         compiler_params=pltpu.CompilerParams(vmem_limit_bytes=16 << 20),
         cost_estimate=pl.CostEstimate(flops=1_000_000, bytes_accessed=1_000, transcendentals=0),
         name="head",
@@ -297,9 +298,8 @@
 def make_front_kernel(planes, leaves):
     def kernel(
         mask_ref, mine, other, both, both_other, g_s, li_s, rhs_h, rhs_l, auxl_h, auxl_l, xa_h, xa_l,
-        x_h, x_l, t_h, t_l, tl_h, tl_l, base_top, base_leaf, row_h, row_l, col_h, col_l, c_top,
-        b_s, t0_s, am_s, d_s, own,
-        lhs_h, lhs_l, ra_h, ra_l, rq_h, rq_l, aux_h, aux_l, rrs_h, rrs_l,
+        b_s, ra_h, ra_l, aux_h, aux_l, x_h, x_l, t_h, t_l, tl_h, tl_l, base_top, base_leaf, row_h, row_l, col_h, col_l, c_top,
+        t0_s, d_s, own, lhs_h, lhs_l, rq_h, rq_l, rrs_h, rrs_l,
     ):
         device = lax.axis_index("row")
         plane = own_plane(device, planes)
@@ -314,7 +314,6 @@
                 )
         for k, ref in enumerate((mine, other)):
             d_s[:, at((half ^ k) * 64, 64), :] = ref[:, 608:672, :]
-        mid_blocks(planes, mine, other, b_s, am_s, ra_h, ra_l)
         _, pair, swapped = places(planes)
         pair = 1 - pair
         masks = [mask_ref[pl.ds(pair * 2 + e, 1), :] for e in (0, 1)]
@@ -334,7 +333,6 @@
         put_pair(lhs_h, lhs_l, 384, 0, q_r, q_i)
         put_pair(lhs_h, lhs_l, 256, 256, q_r.T, q_i.T)
         put_rhs(rq_h, rq_l, 0, q_r, q_i)
-        put_pair(aux_h, aux_l, 0, 0, am_s[0].T, am_s[1].T)
         got = mm3(aux_h[...], aux_l[...], rq_h[...], rq_l[...])
         d_r, d_i = d_s[0] - got[:, 0:128], d_s[1] - got[:, 128:256]
         put_pair(lhs_h, lhs_l, 256, 0, d_r, d_i)
@@ -388,18 +386,17 @@
     return pl.pallas_call(
         make_front_kernel(planes, leaves),
         out_shape=tuple(jax.ShapeDtypeStruct(s, d) for s, d in out),
-        in_specs=[VMEM] * 13,
+        in_specs=[VMEM] * 18,
         out_specs=(VMEM,) * len(out),
         scratch_shapes=[
-            v((2, 512, 128), F32),
-            v((2, 128, 128), F32), v((2, 128, 128), F32), v((2, 128, 128), F32),
-            v((2, 128, 512), F32), *pair(512, 512), *pair(256, 256), *pair(256, 256), *pair(128, 256),
+            v((2, 128, 128), F32), v((2, 128, 128), F32),
+            v((2, 128, 512), F32), *pair(512, 512), *pair(256, 256),
             *pair(leaves, 512, 256),
         ],
         compiler_params=pltpu.CompilerParams(vmem_limit_bytes=16 << 20),
         cost_estimate=pl.CostEstimate(flops=1_000_000, bytes_accessed=1_000, transcendentals=0),
         name="front",
-    )(masks, *pieces, *prepared, *heads[:2])
+    )(masks, *pieces, *prepared, *heads[:2], *heads[6:])
 
 
 def own_product(planes, row_h, row_l, col_h, col_l, *xs):
@@ -442,15 +439,22 @@
         for k, ref in enumerate((b0, b1, b2, b3)):
             for n in range(6):
                 blocks[n, :, at((quarter ^ k) * 32, 32), :] = ref[:, n * 32 : n * 32 + 32, :]
+        held = {}
         for n, (row, col) in enumerate(((1, 1), (1, 2), (1, 3), (2, 2), (3, 3), (3, 2))):
             re, im = blocks[n, 0], blocks[n, 1]
-            put_pair(a_h, a_l, row * 128 - 128, col * 256 - 256, re, im)
+            held[row, col] = (re, im)
             if row != col:
-                put_pair(a_h, a_l, col * 128 - 128, row * 256 - 256, re.T, im.T)
+                held[col, row] = (re.T, im.T)
+        for row in (1, 2, 3):
+            one, three = held[row, 1], held[row, 3]
+            first = [jnp.where(near, x, y) for x, y in zip(one, three)]
+            second = [jnp.where(near, y, x) for x, y in zip(one, three)]
+            for place, (re, im) in enumerate((first, second, held[row, 2])):
+                put_pair(a_h, a_l, row * 128 - 128, place * 256, re, im)
 
         def columns(j, out):
-            xh = jnp.concatenate([pick(near, r, xa_h, xb_h, j) for r in (1, 2, 3)], axis=0)
-            xl = jnp.concatenate([pick(near, r, xa_l, xb_l, j) for r in (1, 2, 3)], axis=0)
+            xh = jnp.concatenate([xa_h[j, 256:512], xb_h[j, 256:512], pick(near, 2, xa_h, xb_h, j)], axis=0)
+            xl = jnp.concatenate([xa_l[j, 256:512], xb_l[j, 256:512], pick(near, 2, xa_l, xb_l, j)], axis=0)
             got = mm3(a_h[...], a_l[...], xh, xl)
             for r in range(4):
                 rows = slice(r * 128, r * 128 + 128)
@@ -588,7 +592,7 @@
         far = stack(*far)
         root = [both, pieces[3], far, swap(far, 1)]
     c_leaf = own_product(planes, *firsts[8:12], *heads[:2], *firsts[:2])
-    return back(planes, masks, root, [*heads, *firsts[:8], firsts[12], c_leaf], leaves)
+    return back(planes, masks, root, [*heads[:6], *firsts[:8], firsts[12], c_leaf], leaves)
 
 
 def solution(mesh):

time: 27.8 us -> 27.6 us (level)
  no operation moved by 1% of the time
where the time goes in v4:
time: 27.6 us; the launch traced here: 27.5 us
  Pallas kernels  15.1 us (55%)
  starting transfers between devices  9.09 us (33%)
  waiting for transfers between devices  2.51 us (9%)
  between operations  0.74 us (3%)
    ppermute x9, starting transfers between devices, swap(): lax.ppermute(x, 'row', [(i, i ^ apart) for i in range(lax.axis_size('row'...  9.09 us
    pallas_call x1, Pallas kernels, back(): pl.pallas_call(make_back_kernel(planes, leaves), out_shape=tuple((jax.Sha...  6.12 us
    pallas_call x1, Pallas kernels, front(): pl.pallas_call(make_front_kernel(planes, leaves), out_shape=tuple((jax.Sh...  3.41 us
    ppermute x9, waiting for transfers between devices, swap(): lax.ppermute(x, 'row', [(i, i ^ apart) for i in range(lax.axis_size('row'...  2.51 us
    pallas_call x1, Pallas kernels, prep(): pl.pallas_call(make_prep_kernel(leaves), out_shape=tuple((jax.ShapeDtypeS...  1.74 us
    pallas_call x1, Pallas kernels, head(): pl.pallas_call(make_head_kernel(planes), out_shape=tuple((jax.ShapeDtypeS...  1.35 us
    pallas_call x1, Pallas kernels, own_product(): pl.pallas_call(kernel, out_shape=jax.ShapeDtypeStruct((xs[0].shape[0] - 2...  1.27 us
    pallas_call x1, Pallas kernels, pack(): pl.pallas_call(pack_kernel, out_shape=tuple((jax.ShapeDtypeStruct(s, F32)...  1.17 us
  transfers between devices with their start and end apart: 9, of which 2 were waited for; matrix products, arithmetic and copies ran while one was open for 0% of the time, Pallas kernels for 28%

profile of v4, /device:TPU:0, one launch (start us, length us, event | category | flops | bytes accessed | tf_op | source)
XLA Modules:
  0.0 27.5 jit_solution(12792288931873746463)
XLA Ops:
  0.6 1.2 %pack_panels.1 = (f32[2,288,128]{2,1,0:T(8,128)S(1)}, f32[2,672,128]{2,1,0:T(8,128)S(1)}, f32[8,128]{1,0:T(8,128)S(1)}, f32[2,96,128]{2,1,0:T(8,128)S(1)}, f32[2...) custom-call(s32[4,4]{1,0:T(4,128)} %pat.1, f32[2,32,512]{2,1,0:T(8,128)} %a_hbm.1, f32[2,128,128]{2,1,0:T(8,128)} %t_hbm.1, ...), custom_call_target="tpu_custom_call" | custom-call | flops 1000000 | bytes 1000 | tf_op jit(solution)/shard_map/pack_panels/pallas_call | solution.py:75
  1.8 0.5 %collective-permute-start.3 = (f32[2,672,128]{2,1,0:T(8,128)S(1)}, f32[2,672,128]{2,1,0:T(8,128)S(1)}, u32[]{:S(2)}, u32[]{:S(2)}) collective-permute-start(f32[2,672,128]{2,1,0:T(8,128)S(1)} %get-tuple-element.70.mine), channel_id=1, source_target_pairs={{0,1},{1,0},{2,3},{3,2},{4,5},{5,4},{6,7},{7,6},{8,9},{9,8},{10,11... | collective-permute-start | bytes 2064392 | tf_op jit(solution)/shard_map/ppermute | solution.py:15
  2.3 2.6 %collective-permute-start.4 = (f32[2,288,128]{2,1,0:T(8,128)S(1)}, f32[2,288,128]{2,1,0:T(8,128)S(1)}, u32[]{:S(2)}, u32[]{:S(2)}) collective-permute-start(f32[2,288,128]{2,1,0:T(8,128)S(1)} %get-tuple-element.88), channel_id=1, source_target_pairs={{0,2},{1,3},{2,0},{3,1},{4,6},{5,7},{6,4},{7,5},{8,10},{9,11},{10,... | collective-permute-start | bytes 884744 | tf_op jit(solution)/shard_map/ppermute | solution.py:15
  4.9 1.6 %collective-permute-start = (f32[2,96,128]{2,1,0:T(8,128)S(1)}, f32[2,96,128]{2,1,0:T(8,128)S(1)}, u32[]{:S(2)}, u32[]{:S(2)}) collective-permute-start(f32[2,96,128]{2,1,0:T(8,128)S(1)} %get-tuple-element.67), channel_id=1, source_target_pairs={{0,4},{1,5},{2,6},{3,7},{4,0},{5,1},{6,2},{7,3},{8,12},{9,13},{10,... | collective-permute-start | bytes 294920 | tf_op jit(solution)/shard_map/ppermute | solution.py:15
  6.5 2.5 %collective-permute-start.2 = (f32[2,64,128]{2,1,0:T(8,128)S(1)}, f32[2,64,128]{2,1,0:T(8,128)S(1)}, u32[]{:S(2)}, u32[]{:S(2)}) collective-permute-start(f32[2,64,128]{2,1,0:T(8,128)S(1)} %get-tuple-element.69), channel_id=1, source_target_pairs={{0,12},{1,13},{2,14},{3,15},{4,8},{5,9},{6,10},{7,11},{8,4},{9,5},... | collective-permute-start | bytes 196616 | tf_op jit(solution)/shard_map/ppermute | solution.py:15
  9.0 0.1 collective-permute-start.1
  9.1 1.7 %prep.1 = (f32[2,1536,128]{2,1,0:T(8,128)S(1)}, f32[2,384,128]{2,1,0:T(8,128)S(1)}, bf16[3,512,256]{2,1,0:T(8,128)(2,1)S(1)}, bf16[3,512,256]{2,1,0:T(8,128)(2,1...) custom-call(f32[2,1536,128]{2,1,0:T(8,128)} %panel.1, f32[2,384,128]{2,1,0:T(8,128)} %link_c.1, ...), custom_call_target="tpu_custom_call" | custom-call | flops 1000000 | bytes 1000 | tf_op jit(solution)/shard_map/prep/pallas_call | solution.py:180
  10.9 0.0 collective-permute-done.3.other
  10.9 1.4 %head.1 = (bf16[5,512,256]{2,1,0:T(8,128)(2,1)S(1)}, bf16[5,512,256]{2,1,0:T(8,128)(2,1)S(1)}, bf16[512,256]{1,0:T(8,128)(2,1)S(1)}, bf16[512,256]{1,0:T(8,128)(...) custom-call(f32[8,128]{1,0:T(8,128)S(1)} %get-tuple-element.66.mask_, ...), custom_call_target="tpu_custom_call" | custom-call | flops 1000000 | bytes 1000 | tf_op jit(solution)/shard_map/head/pallas_call | solution.py:268
  12.2 2.2 %collective-permute-done.1.z2 = f32[2,32,128]{2,1,0:T(8,128)S(1)} collective-permute-done((f32[2,32,128]{2,1,0:T(8,128)S(1)}, f32[2,32,128]{2,1,0:T(8,128)S(1)}, u32[]{:S(2)}, u32[]{:S(2)}) %collective-permute-start.1) | collective-permute-done | bytes 32800 | tf_op jit(solution)/shard_map/ppermute | solution.py:15
  14.4 0.0 collective-permute-done.2.z3
  14.4 0.0 collective-permute-done.z1
  14.4 0.0 collective-permute-done.4.far_top
  14.4 0.1 collective-permute-start.5
  14.5 0.3 %collective-permute-start.6 = (f32[2,96,128]{2,1,0:T(8,128)S(1)}, f32[2,96,128]{2,1,0:T(8,128)S(1)}, u32[]{:S(2)}, u32[]{:S(2)}) collective-permute-start(f32[2,96,128]{2,1,0:T(8,128)S(1)} %get-tuple-element.90), channel_id=1, source_target_pairs={{0,4},{1,5},{2,6},{3,7},{4,0},{5,1},{6,2},{7,3},{8,12},{9,13},{10,... | collective-permute-start | bytes 294920 | tf_op jit(solution)/shard_map/ppermute | solution.py:15
  14.8 1.3 %collective-permute-start.7 = (f32[2,96,128]{2,1,0:T(8,128)S(1)}, f32[2,96,128]{2,1,0:T(8,128)S(1)}, u32[]{:S(2)}, u32[]{:S(2)}) collective-permute-start(f32[2,96,128]{2,1,0:T(8,128)S(1)} %get-tuple-element.91), channel_id=1, source_target_pairs={{0,2},{1,3},{2,0},{3,1},{4,6},{5,7},{6,4},{7,5},{8,10},{9,11},{10,... | collective-permute-start | bytes 294920 | tf_op jit(solution)/shard_map/ppermute | solution.py:15
  16.1 0.3 %collective-permute-done.5.both_other.b1 = f32[2,480,128]{2,1,0:T(8,128)S(1)} collective-permute-done((f32[2,480,128]{2,1,0:T(8,128)S(1)}, f32[2,480,128]{2,1,0:T(8,128)S(1)}, u32[]{:S(2)}, u32[]{:S(2)}) %collective-permute-start.5) | collective-permute-done | bytes 491552 | tf_op jit(solution)/shard_map/ppermute | solution.py:15
  16.4 3.4 %front.1 = (bf16[5,512,256]{2,1,0:T(8,128)(2,1)S(1)}, bf16[5,512,256]{2,1,0:T(8,128)(2,1)S(1)}, bf16[512,256]{1,0:T(8,128)(2,1)S(1)}, bf16[512,256]{1,0:T(8,128)...) custom-call(f32[8,128]{1,0:T(8,128)S(1)} %get-tuple-element.66.mask_, ...), custom_call_target="tpu_custom_call" | custom-call | flops 1000000 | bytes 1000 | tf_op jit(solution)/shard_map/front/pallas_call | solution.py:386
  19.8 0.0 collective-permute-done.6.upper
  19.8 0.0 collective-permute-done.7.lower
  19.8 0.2 collective-permute-start.8
  20.0 1.3 %own_product.1.c_leaf = f32[3,512,256]{2,1,0:T(8,128)S(1)} custom-call(bf16[128,1024]{1,0:T(8,128)(2,1)S(1)} %get-tuple-element.119.row_h, bf16[128,1024]{1,0:T(8,128)(2,1)S(1)} %get-tuple-element.120.row_l, bf16[384,256]{1,0:T(8,128)(2,1)S(1)} %get-tuple-element.121.col_h, bf16[384,256]{1,0:T(8,128)(2,1)S(1)} %get-tuple-element.122.col_l, ...), custom_call_target="tpu_custom_call" | custom-call | flops 1000000 | bytes 1000 | tf_op jit(solution)/shard_map/own_product/pallas_call | solution.py:407
  21.3 0.0 collective-permute-done.8.b3
  21.3 6.1 %back.1 = (f32[2,128,128]{2,1,0:T(8,128)}, f32[2,32,128]{2,1,0:T(8,128)}, f32[2,256,128]{2,1,0:T(8,128)}, f32[2,64,128]{2,1,0:T(8,128)}, f32[2,64,128]{2,1,0:T(8...) custom-call(f32[8,128]{1,0:T(8,128)S(1)} %get-tuple-element.66.mask_r, ...), custom_call_target="tpu_custom_call" | custom-call | flops 8000000000 | bytes 12000000 | tf_op jit(solution)/shard_map/back/pallas_call | solution.py:529
  (2 shorter events, 0.1 us)
Async XLA Ops:
  1.8 9.0 %collective-permute-start.3 = (f32[2,672,128]{2,1,0:T(8,128)S(1)}, f32[2,672,128]{2,1,0:T(8,128)S(1)}, u32[]{:S(2)}, u32[]{:S(2)}) collective-permute-start(f32[2,672,128]{2,1,0:T(8,128)S(1)} %get-tuple-element.70.mine), channel_id=1, source_target_pairs={{0,1},{1,0},{2,3},{3,2},{4,5},{5,4},{6,7},{7,6},{8,9},{9,8},{10,11... | collective-permute-start | bytes 2064392 | tf_op jit(solution)/shard_map/ppermute | solution.py:15
  2.3 12.0 %collective-permute-start.4 = (f32[2,288,128]{2,1,0:T(8,128)S(1)}, f32[2,288,128]{2,1,0:T(8,128)S(1)}, u32[]{:S(2)}, u32[]{:S(2)}) collective-permute-start(f32[2,288,128]{2,1,0:T(8,128)S(1)} %get-tuple-element.88), channel_id=1, source_target_pairs={{0,2},{1,3},{2,0},{3,1},{4,6},{5,7},{6,4},{7,5},{8,10},{9,11},{10,... | collective-permute-start | bytes 884744 | tf_op jit(solution)/shard_map/ppermute | solution.py:15
  4.9 9.4 %collective-permute-start = (f32[2,96,128]{2,1,0:T(8,128)S(1)}, f32[2,96,128]{2,1,0:T(8,128)S(1)}, u32[]{:S(2)}, u32[]{:S(2)}) collective-permute-start(f32[2,96,128]{2,1,0:T(8,128)S(1)} %get-tuple-element.67), channel_id=1, source_target_pairs={{0,4},{1,5},{2,6},{3,7},{4,0},{5,1},{6,2},{7,3},{8,12},{9,13},{10,... | collective-permute-start | bytes 294920 | tf_op jit(solution)/shard_map/ppermute | solution.py:15
  6.5 7.9 %collective-permute-start.2 = (f32[2,64,128]{2,1,0:T(8,128)S(1)}, f32[2,64,128]{2,1,0:T(8,128)S(1)}, u32[]{:S(2)}, u32[]{:S(2)}) collective-permute-start(f32[2,64,128]{2,1,0:T(8,128)S(1)} %get-tuple-element.69), channel_id=1, source_target_pairs={{0,12},{1,13},{2,14},{3,15},{4,8},{5,9},{6,10},{7,11},{8,4},{9,5},... | collective-permute-start | bytes 196616 | tf_op jit(solution)/shard_map/ppermute | solution.py:15
  9.0 5.4 %collective-permute-start.1 = (f32[2,32,128]{2,1,0:T(8,128)S(1)}, f32[2,32,128]{2,1,0:T(8,128)S(1)}, u32[]{:S(2)}, u32[]{:S(2)}) collective-permute-start(f32[2,32,128]{2,1,0:T(8,128)S(1)} %get-tuple-element.68), channel_id=1, source_target_pairs={{0,8},{1,9},{2,10},{3,11},{4,12},{5,13},{6,14},{7,15},{8,0},{9,1},... | collective-permute-start | bytes 98312 | tf_op jit(solution)/shard_map/ppermute | solution.py:15
  14.4 1.9 %collective-permute-start.5 = (f32[2,480,128]{2,1,0:T(8,128)S(1)}, f32[2,480,128]{2,1,0:T(8,128)S(1)}, u32[]{:S(2)}, u32[]{:S(2)}) collective-permute-start(f32[2,480,128]{2,1,0:T(8,128)S(1)} %get-tuple-element.89.both.b0), channel_id=1, source_target_pairs={{0,1},{1,0},{2,3},{3,2},{4,5},{5,4},{6,7},{7,6},{8,9},{9,8},{10,11... | collective-permute-start | bytes 1474568 | tf_op jit(solution)/shard_map/ppermute | solution.py:15
  14.5 5.3 %collective-permute-start.6 = (f32[2,96,128]{2,1,0:T(8,128)S(1)}, f32[2,96,128]{2,1,0:T(8,128)S(1)}, u32[]{:S(2)}, u32[]{:S(2)}) collective-permute-start(f32[2,96,128]{2,1,0:T(8,128)S(1)} %get-tuple-element.90), channel_id=1, source_target_pairs={{0,4},{1,5},{2,6},{3,7},{4,0},{5,1},{6,2},{7,3},{8,12},{9,13},{10,... | collective-permute-start | bytes 294920 | tf_op jit(solution)/shard_map/ppermute | solution.py:15
  14.8 5.0 %collective-permute-start.7 = (f32[2,96,128]{2,1,0:T(8,128)S(1)}, f32[2,96,128]{2,1,0:T(8,128)S(1)}, u32[]{:S(2)}, u32[]{:S(2)}) collective-permute-start(f32[2,96,128]{2,1,0:T(8,128)S(1)} %get-tuple-element.91), channel_id=1, source_target_pairs={{0,2},{1,3},{2,0},{3,1},{4,6},{5,7},{6,4},{7,5},{8,10},{9,11},{10,... | collective-permute-start | bytes 294920 | tf_op jit(solution)/shard_map/ppermute | solution.py:15
  19.8 1.5 %collective-permute-start.8 = (f32[2,192,128]{2,1,0:T(8,128)S(1)}, f32[2,192,128]{2,1,0:T(8,128)S(1)}, u32[]{:S(2)}, u32[]{:S(2)}) collective-permute-start(f32[2,192,128]{2,1,0:T(8,128)S(1)} %stack_root.1.b2), channel_id=1, source_target_pairs={{0,1},{1,0},{2,3},{3,2},{4,5},{5,4},{6,7},{7,6},{8,9},{9,8},{10,11... | collective-permute-start | bytes 589832 | tf_op jit(solution)/shard_map/ppermute | solution.py:15
